TPU v7x, 32 devices: a whole 2x2x4 slice. The times are simulated.
32 devices in a mesh: grp: 4 (over x, core), sub: 8 (over z, y).
Axes of the slice: x: 2, y: 2, z: 4, core: 2. Of those that a mesh axis runs over, the one named last changes fastest.
Arguments:
- right_side: float32 [65536, 128], P(('grp', 'sub')), may hold values from -6 to 6
- fine_values: float32 [81, 65536], P(None, ('grp', 'sub')), as said below
- columns: int32 [81, 65536], P(None, ('grp', 'sub')), may hold values from 0 to 2175, as said below
- agg_map: int32 [65536], P(('grp', 'sub')), may hold values from 0 to 127
- send_lo: int32 [2048], P(('grp', 'sub')), may hold values from 0 to 2047
- send_hi: int32 [2048], P(('grp', 'sub')), may hold values from 0 to 2047
- coarse_matrix: float32 [4, 1024, 1024], P('grp', 'sub'), as said below
Outputs:
- solution: float32 [65536, 128], P(('grp', 'sub'))
- residual: float32 [65536, 128], P(('grp', 'sub'))
Inputs may be any that keep to these rules, and one draw needn't show every extreme that they name: `columns`: entry 0 of row i of a partition is 64 + i, the others lie within 64 positions of it. `fine_values`: entry 0 lies in 2.5 to 5 and every other entry's magnitude is at most 0.06. `coarse_matrix`: symmetric; the diagonal lies in 10 to 20, other entries' magnitudes are at most 7.1 / sqrt(1024).
All inputs are finite; a program needn't handle non-finite values.
Results may differ from a plain program's by a relative error of at most 0.0001.
Values sent between devices are 32-bit elements; how exact they have to be, the bound alone decides.
A program may use at most 128 MiB of HBM per device.

v0:
```python
import functools

import jax
import jax.numpy as jnp
from jax import lax
from jax.experimental import pallas as pl
from jax.experimental.pallas import tpu as pltpu
from jax.sharding import PartitionSpec as P

CHEB_FINE = 2
CHEB_COARSE = 6
CYCLES = 2
APPLIES = 7

THETA = 1.0
DELTA = 0.7
OMEGA = 0.6
MESH = pl.DeviceIdType.MESH
f32 = jnp.float32
bf16 = jnp.bfloat16


def split(x):
    hi = x.astype(bf16)
    lo = (x - hi.astype(f32)).astype(bf16)
    return hi, lo


def iota(shape, dim):
    return lax.broadcasted_iota(jnp.int32, shape, dim)


def setup_kernel(fv_ref, col_ref, agg_ref, a_ref, dinv_ref, diag_ref, oht_ref, oh_ref):
    block = fv_ref.shape[1]
    count = fv_ref.shape[0] - 1
    groups = count // 8
    base = pl.program_id(0) * block
    rows = iota((8, block), 1)
    cols, vals, firsts = [], [], []
    for i in range(groups):
        cols.append(col_ref[1 + 8 * i : 9 + 8 * i, :] - base - rows)
        vals.append(fv_ref[1 + 8 * i : 9 + 8 * i, :])
    last = jnp.zeros((8, block), f32)
    for i in range(groups):
        last = last + jnp.where(cols[i] == block, vals[i], 0.0)
    last = jnp.sum(last, axis=0, keepdims=True)
    for j in range(groups):
        total = vals[j]
        for i in range(j + 1, groups):
            total = total + jnp.where(cols[i] == cols[j], vals[i], 0.0)
        firsts.append(total)
    high_count = block // 8
    places = [iota((8, block), 0) + 8 * h for h in range(high_count)]
    sums = [jnp.zeros((8, block), f32)] * high_count
    for s in range(8):
        chains = [jnp.zeros((8, block), f32)] * high_count
        for i in reversed(range(groups)):
            col = jnp.broadcast_to(cols[i][s : s + 1, :], (8, block))
            val = jnp.broadcast_to(firsts[i][s : s + 1, :], (8, block))
            chains = [jnp.where(col == places[h], val, chains[h]) for h in range(high_count)]
        sums = [sums[h] + chains[h] for h in range(high_count)]
    by_offset = jnp.concatenate(sums, axis=0).T
    skewed = pltpu.roll(by_offset, 0, 1, stride=1, stride_axis=0)
    lane = iota((block, block), 1)
    sub = iota((block, block), 0)
    low = jnp.where(lane >= sub, skewed, 0.0)
    high = jnp.where(lane < sub, skewed, jnp.where(lane == sub, last, 0.0))
    for part, at in ((low, 0), (high, block)):
        hi, lo = split(part)
        a_ref[:block, at : at + block] = hi
        a_ref[block:, at : at + block] = lo
    diag = jnp.broadcast_to(fv_ref[0:1, :], (block, block)).T
    diag_ref[...] = diag
    dinv_ref[...] = 1.0 / diag
    count_agg = oht_ref.shape[0]
    onehot = (iota((count_agg, block), 0) == agg_ref[...]).astype(f32)
    oht_ref[...] = onehot.astype(bf16)
    oh_ref[...] = onehot.T.astype(bf16)


def run_setup(fine_values, columns, agg_map, block, aggregates):
    entries, rows = fine_values.shape
    blocks = rows // block
    return pl.pallas_call(
        setup_kernel,
        grid=(blocks,),
        in_specs=[
            pl.BlockSpec((entries, block), lambda b: (0, b)),
            pl.BlockSpec((entries, block), lambda b: (0, b)),
            pl.BlockSpec((1, block), lambda b: (0, b)),
        ],
        out_specs=[
            pl.BlockSpec((2 * block, 2 * block), lambda b: (b, 0)),
            pl.BlockSpec((block, block), lambda b: (b, 0)),
            pl.BlockSpec((block, block), lambda b: (b, 0)),
            pl.BlockSpec((aggregates, block), lambda b: (0, b)),
            pl.BlockSpec((block, aggregates), lambda b: (b, 0)),
        ],
        out_shape=[
            jax.ShapeDtypeStruct((2 * rows, 2 * block), bf16),
            jax.ShapeDtypeStruct((rows, block), f32),
            jax.ShapeDtypeStruct((rows, block), f32),
            jax.ShapeDtypeStruct((aggregates, rows), bf16),
            jax.ShapeDtypeStruct((rows, aggregates), bf16),
        ],
        cost_estimate=pl.CostEstimate(flops=10_000_000_000, bytes_accessed=50_000_000, transcendentals=0),
        name="setup",
    )(fine_values, columns, agg_map.reshape(1, rows))


def poly_kernel(m_ref, out_ref, m_hi, m_lo, d_ref, z_ref, x_ref, pair):
    coarse = m_ref.shape[0]
    agg = x_ref.shape[0]
    parts = coarse // agg
    half = parts // 2
    me = lax.axis_index("sub")
    eye = iota((agg, agg), 0) == iota((agg, agg), 1)
    cinv = []
    for j in range(coarse // agg):
        sl = slice(j * agg, (j + 1) * agg)
        cinv.append(1.0 / jnp.sum(jnp.where(eye, m_ref[sl, :agg], 0.0), axis=0, keepdims=True))
        for k in range(half + 1):
            other = (j + k) % parts
            so = slice(other * agg, (other + 1) * agg)
            tile = m_ref[sl, k * agg : (k + 1) * agg]
            m_hi[sl, so], m_lo[sl, so] = split(tile)
            if 0 < k and 2 * k < parts:
                m_hi[so, sl], m_lo[so, sl] = split(tile.T)
    for j in range(coarse // agg):
        sl = slice(j * agg, (j + 1) * agg)
        start = jnp.where(jnp.logical_and(eye, me == j), cinv[j], 0.0)
        d_ref[:, sl] = start
        z_ref[:, sl] = start
        x_ref[:, sl] = start
    rho_old = DELTA / THETA
    for turn in range(1, CHEB_COARSE):
        rho_new = 1.0 / (2.0 * THETA / DELTA - rho_old)
        hi, lo = split(d_ref[...])
        pair[:agg, :] = hi
        pair[agg:, :] = lo
        for j in range(coarse // agg // 2):
            sl = slice(2 * j * agg, (2 * j + 2) * agg)
            both = jnp.dot(pair[...], m_hi[:, sl], preferred_element_type=f32)
            low = jnp.dot(pair[:agg, :], m_lo[:, sl], preferred_element_type=f32)
            scale = jnp.concatenate([cinv[2 * j], cinv[2 * j + 1]], axis=1)
            z = z_ref[:, sl] - (both[:agg] + (both[agg:] + low)) * scale
            d = rho_new * rho_old * d_ref[:, sl] + (2.0 * rho_new / DELTA) * z
            z_ref[:, sl] = z
            d_ref[:, sl] = d
            x_ref[:, sl] += d
        rho_old = rho_new
    hi, lo = split(x_ref[...])
    out_ref[:agg, :] = hi
    out_ref[agg:, :] = lo


def run_poly(matrix, agg):
    coarse = matrix.shape[0]
    vmem = pl.BlockSpec(memory_space=pltpu.VMEM)
    return pl.pallas_call(
        poly_kernel,
        in_specs=[vmem],
        out_specs=vmem,
        out_shape=jax.ShapeDtypeStruct((2 * agg, coarse), bf16),
        scratch_shapes=[
            pltpu.VMEM((coarse, coarse), bf16),
            pltpu.VMEM((coarse, coarse), bf16),
            pltpu.VMEM((agg, coarse), f32),
            pltpu.VMEM((agg, coarse), f32),
            pltpu.VMEM((agg, coarse), f32),
            pltpu.VMEM((2 * agg, coarse), bf16),
        ],
        compiler_params=pltpu.CompilerParams(vmem_limit_bytes=50 * 1024 * 1024),
        name="poly",
    )(matrix)


def quads(product, rows, width):
    return product[:rows, :width] + (product[:rows, width:] + product[rows:, :width])


def main_kernel(opening, n_grp, n_sub, *refs):
    if opening:
        (rhs_ref, a_ref, dinv_ref, oht_ref, lo_ref, hi_ref,
         sol_ref, res_ref, crhs_ref,
         xs, ext, s2, send, recv, send_sem, recv_sem) = refs
        agg = oht_ref.shape[0]
    else:
        (sol_in, rhs_ref, crhs_ref, a_ref, dinv_ref, diag_ref, oht_ref, oh_ref, lo_ref, hi_ref, m2,
         sol_ref, res_ref,
         xs, ext, s2, send, recv, send_sem, recv_sem,
         csend, whole, csend_sem, crecv_sem) = refs
        agg = oht_ref.shape[0]
    rows_dev, width = rhs_ref.shape
    ghost = lo_ref.shape[0]
    block = 2 * ghost
    blocks = rows_dev // block
    grp = lax.axis_index("grp")
    me = lax.axis_index("sub")
    part = grp * n_sub + me
    has_next = part < n_grp * n_sub - 1
    has_prev = part > 0
    after, before = part + 1, part - 1
    next_id = (lax.div(after, n_sub), lax.rem(after, n_sub))
    prev_id = (lax.div(before, n_sub), lax.rem(before, n_sub))
    cross_next = jnp.logical_and(has_next, me == n_sub - 1)
    cross_prev = jnp.logical_and(has_prev, me == 0)

    barrier = pltpu.get_barrier_semaphore()
    if opening:
        greet_next, greet_prev, greeted = has_next, has_prev, 0
    else:
        greet_next, greet_prev, greeted = cross_next, cross_prev, n_sub - 1
        for j in range(1, n_sub):
            pl.semaphore_signal(barrier, inc=1, device_id=(grp, lax.rem(me + j, n_sub)), device_id_type=MESH)

    @pl.when(greet_next)
    def _():
        pl.semaphore_signal(barrier, inc=1, device_id=next_id, device_id_type=MESH)

    @pl.when(greet_prev)
    def _():
        pl.semaphore_signal(barrier, inc=1, device_id=prev_id, device_id_type=MESH)

    mine = pl.multiple_of(me * agg, agg)
    ext[:ghost, :] = jnp.zeros((ghost, 2 * width), bf16)
    ext[ghost + rows_dev :, :] = jnp.zeros((ghost, 2 * width), bf16)

    def each_block(fn):
        def go(b, carry):
            fn(pl.ds(pl.multiple_of(b * block, block), block))
            return carry
        lax.fori_loop(0, blocks, go, 0, unroll=True)

    def first(sl):
        rhs = rhs_ref[sl, :]
        res_ref[sl, :] = rhs
        if opening:
            sol_ref[sl, :] = jnp.zeros_like(rhs)
            xs[0, sl, :] = dinv_ref[sl, :] * rhs
        else:
            sol_ref[sl, :] = sol_in[sl, :]

    each_block(first)
    pl.semaphore_wait(barrier, greeted + greet_next.astype(jnp.int32) + greet_prev.astype(jnp.int32))

    def halo_copy(ex, way, device):
        return pltpu.make_async_remote_copy(
            src_ref=send.at[ex, way], dst_ref=recv.at[ex, way],
            send_sem=send_sem.at[ex, way], recv_sem=recv_sem.at[ex, way],
            device_id=device, device_id_type=MESH,
        )

    def apply(ex, cur, epilogue):
        up = halo_copy(ex, 0, next_id)
        down = halo_copy(ex, 1, prev_id)

        @pl.when(has_next)
        def _():
            def pick(i, carry):
                for k in range(16):
                    send[ex, 0, pl.ds(16 * i + k, 1), :] = xs[cur, pl.ds(hi_ref[16 * i + k], 1), :]
                return carry

            lax.fori_loop(0, ghost // 16, pick, 0)
            up.start()

        @pl.when(has_prev)
        def _():
            def pick(i, carry):
                for k in range(16):
                    send[ex, 1, pl.ds(16 * i + k, 1), :] = xs[cur, pl.ds(lo_ref[16 * i + k], 1), :]
                return carry

            lax.fori_loop(0, ghost // 16, pick, 0)
            down.start()

        for b in range(blocks):
            hi, lo = split(xs[cur, b * block : (b + 1) * block, :])
            at = ghost + b * block
            ext[at : at + block, :width] = hi
            ext[at : at + block, width:] = lo

        def one(b):
            a = a_ref[pl.ds(pl.multiple_of(b * 2 * block, 2 * block), 2 * block), :]
            x = ext[pl.ds(pl.multiple_of(b * block, block), 2 * block), :]
            off = quads(jnp.dot(a, x, preferred_element_type=f32), block, width)
            epilogue(pl.ds(pl.multiple_of(b * block, block), block), off)

        def go(b, carry):
            one(1 + 2 * b)
            one(2 + 2 * b)
            return carry

        lax.fori_loop(0, (blocks - 2) // 2, go, 0)

        @pl.when(has_next)
        def _():
            down.wait_recv()
            hi, lo = split(recv[ex, 1])
            ext[ghost + rows_dev :, :width] = hi
            ext[ghost + rows_dev :, width:] = lo
            up.wait_send()

        @pl.when(has_prev)
        def _():
            up.wait_recv()
            hi, lo = split(recv[ex, 0])
            ext[:ghost, :width] = hi
            ext[:ghost, width:] = lo
            down.wait_send()

        one(0)
        one(blocks - 1)

    def gather(step):
        half = n_sub // 2
        partner = me + 1 - 2 * lax.rem(me, 2)

        def block_copy(source, origin, slot, peer):
            return pltpu.make_async_remote_copy(
                src_ref=source, dst_ref=whole.at[step, pl.ds(pl.multiple_of(origin * agg, agg), agg)],
                send_sem=csend_sem.at[step, slot], recv_sem=crecv_sem.at[step, slot],
                device_id=(grp, peer), device_id_type=MESH,
            )

        copies = [block_copy(csend.at[step], me, 0, partner)]
        for j in range(1, half):
            copies.append(block_copy(csend.at[step], me, j, lax.rem(me + 2 * j, n_sub)))
        for copy in copies:
            copy.start()
        whole[step, pl.ds(mine, agg), :] = csend[step]
        passed = []
        for j in range(1, half):
            copies[j].wait_recv()
            origin = lax.rem(me + n_sub - 2 * j, n_sub)
            block_ref = whole.at[step, pl.ds(pl.multiple_of(origin * agg, agg), agg)]
            copy = block_copy(block_ref, origin, half + j, partner)
            copy.start()
            passed.append(copy)
        copies[0].wait_recv()
        for copy in passed:
            copy.wait_recv()
        for copy in copies + passed:
            copy.wait_send()
        hi, lo = split(whole[step])
        x = jnp.concatenate([hi, lo], axis=1)
        return quads(jnp.dot(m2[...], x, preferred_element_type=f32), agg, width)

    rho0 = DELTA / THETA
    rho1 = 1.0 / (2.0 * THETA / DELTA - rho0)
    c1 = rho1 * rho0
    c2 = 2.0 * rho1 / DELTA

    def smooth(ex):
        def step_one(sl, off):
            d0 = xs[0, sl, :]
            r0 = res_ref[sl, :]
            d1 = c1 * d0 - c2 * dinv_ref[sl, :] * off
            xs[1, sl, :] = d1
            res_ref[sl, :] = (c2 - 1.0) * off - c1 * r0
            sol_ref[sl, :] += d0 + d1

        apply(ex, 0, step_one)

        def step_two(sl, off):
            r = res_ref[sl, :] - off
            res_ref[sl, :] = r
            xs[0, sl, :] = dinv_ref[sl, :] * r

        apply(ex + 1, 1, step_two)

    def restrict(sl, off):
        s = (1.0 - OMEGA) * res_ref[sl, :] - OMEGA * off
        hi, lo = split(s)
        s2[sl, :width] = hi
        s2[sl, width:] = lo

    def restricted(ex):
        apply(ex, 0, restrict)
        both = jnp.dot(oht_ref[...], s2[...], preferred_element_type=f32)
        return both[:, :width] + both[:, width:]

    if opening:
        smooth(0)
        crhs_ref[...] = restricted(2)
        return

    csend[0] = crhs_ref[...]

    def cycle_body(cycle, carry):
        ex = cycle * APPLIES
        hi, lo = split(gather(cycle))
        packed = jnp.concatenate([hi, lo], axis=1)

        def spread(sl):
            both = jnp.dot(oh_ref[sl, :], packed, preferred_element_type=f32)
            xs[0, sl, :] = both[:, :width] + both[:, width:]

        each_block(spread)

        def prolong(sl, off):
            e = (1.0 - OMEGA) * xs[0, sl, :] - OMEGA * (dinv_ref[sl, :] * off)
            xs[1, sl, :] = e
            sol_ref[sl, :] += e

        apply(ex, 0, prolong)

        def correct(sl, off):
            r = res_ref[sl, :] - (diag_ref[sl, :] * xs[1, sl, :] + off)
            res_ref[sl, :] = r
            xs[0, sl, :] = dinv_ref[sl, :] * r

        apply(ex + 1, 1, correct)
        smooth(ex + 2)

        @pl.when(cycle < CYCLES - 1)
        def _():
            smooth(ex + 4)
            csend[cycle + 1] = restricted(ex + 6)

        return carry

    lax.fori_loop(0, CYCLES, cycle_body, 0)


def body(n_grp, n_sub, right_side, fine_values, columns, agg_map, send_lo, send_hi, coarse_matrix):
    rows, width = right_side.shape
    ghost = send_lo.shape[0]
    block = 2 * ghost
    own = coarse_matrix[0]
    agg, coarse = own.shape
    a2, dinv, diag, oht, oh = run_setup(fine_values, columns, agg_map, block, agg)
    start = lax.axis_index("sub") * agg
    kept = (coarse // agg // 2 + 1) * agg
    slab = lax.dynamic_slice_in_dim(jnp.concatenate([own, own], 1), start, kept, 1)
    matrix = lax.all_gather(slab, "sub", axis=0, tiled=True)
    vmem = pl.BlockSpec(memory_space=pltpu.VMEM)
    smem = pl.BlockSpec(memory_space=pltpu.SMEM)
    field = jax.ShapeDtypeStruct((rows, width), f32)

    def scratch(exchanges):
        return [
            pltpu.VMEM((2, rows, width), f32),
            pltpu.VMEM((rows + block, 2 * width), bf16),
            pltpu.VMEM((rows, 2 * width), bf16),
            pltpu.VMEM((exchanges, 2, ghost, width), f32),
            pltpu.VMEM((exchanges, 2, ghost, width), f32),
            pltpu.SemaphoreType.DMA((exchanges, 2)),
            pltpu.SemaphoreType.DMA((exchanges, 2)),
        ]

    def params(number):
        return pltpu.CompilerParams(
            collective_id=number, has_side_effects=True, vmem_limit_bytes=50 * 1024 * 1024
        )

    sol, res, crhs = pl.pallas_call(
        functools.partial(main_kernel, True, n_grp, n_sub),
        in_specs=[vmem] * 4 + [smem] * 2,
        out_specs=[vmem] * 3,
        out_shape=[field, field, jax.ShapeDtypeStruct((agg, width), f32)],
        scratch_shapes=scratch(3),
        compiler_params=params(0),
        cost_estimate=pl.CostEstimate(flops=20_000_000_000, bytes_accessed=60_000_000, transcendentals=0),
        name="opening",
    )(right_side, a2, dinv, oht, send_lo, send_hi)
    p2 = run_poly(matrix, agg)
    return pl.pallas_call(
        functools.partial(main_kernel, False, n_grp, n_sub),
        in_specs=[vmem] * 8 + [smem] * 2 + [vmem],
        out_specs=[vmem] * 2,
        out_shape=[field] * 2,
        scratch_shapes=scratch(CYCLES * APPLIES - 3) + [
            pltpu.VMEM((CYCLES, agg, width), f32),
            pltpu.VMEM((CYCLES, coarse, width), f32),
            pltpu.SemaphoreType.DMA((CYCLES, n_sub)),
            pltpu.SemaphoreType.DMA((CYCLES, n_sub)),
        ],
        compiler_params=params(1),
        name="cycles",
    )(sol, res, crhs, a2, dinv, diag, oht, oh, send_lo, send_hi, p2)


def solution(mesh):
    placed = (
        P(("grp", "sub"), None),
        P(None, ("grp", "sub")),
        P(None, ("grp", "sub")),
        P(("grp", "sub")),
        P(("grp", "sub")),
        P(("grp", "sub")),
        P("grp", "sub", None),
    )
    return jax.shard_map(
        functools.partial(body, mesh.shape["grp"], mesh.shape["sub"]),
        mesh=mesh,
        in_specs=placed,
        out_specs=(P(("grp", "sub"), None), P(("grp", "sub"), None)),
        check_vma=False,
    )
```

profile of v0, /device:TPU:1, one launch (start us, length us, event | category | flops | bytes accessed | tf_op | source)
XLA Modules:
  0.0 159.1 jit_solution(818107915916461572)
XLA Ops:
  7.2 0.0 all-gather.2.cloned.1.call-start
  7.2 1.8 %fusion = f32[128,640]{1,0:T(8,128)} fusion(s32[]{:T(128)S(6)} %select_n.3, f32[128,1024]{1,0:T(8,128)} %bitcast.2), kind=kLoop, calls=%fused_computation.2 | loop fusion | flops 81920 | bytes 851972 | tf_op jit(solution)/shard_map/concatenate | solution.py:436
  9.0 0.0 all-gather.2.cloned.1.call-update
  9.0 0.0 copy-start.6
  9.0 0.0 copy-start.7
  9.0 0.0 copy-start.8
  9.1 14.3 %setup.1 = (bf16[4096,256]{1,0:T(8,128)(2,1)}, f32[2048,128]{1,0:T(8,128)}, f32[2048,128]{1,0:T(8,128)}, bf16[128,2048]{1,0:T(8,128)(2,1)}, bf16[2048,128]{1,0:T(8,128)(2,1)}) custom-call(f32[81,2048]{1,0:T(8,128)} %fv_ref.1, s32[81,2048]{1,0:T(8,128)} %col_ref.1, s32[1,2048]{1,0:T(1,128)} %bitcast.3), custom_call_target="tpu_custom_call" | custom-call | flops 10000000000 | bytes 50000000 | tf_op jit(solution)/shard_map/setup/pallas_call | solution.py:84
  23.4 0.0 copy-done.6
  23.4 0.0 copy-done.7
  23.4 0.0 copy-done.8
  23.4 0.0 copy-start.3
  23.4 1.0 copy-done.3
  24.5 19.8 %opening.1 = (f32[2048,128]{1,0:T(8,128)S(1)}, f32[2048,128]{1,0:T(8,128)S(1)}, f32[128,128]{1,0:T(8,128)S(1)}) custom-call(f32[2048,128]{1,0:T(8,128)S(1)} %copy-done.8, bf16[4096,256]{1,0:T(8,128)(2,1)} %get-tuple-element.10.refs_1_.refs_3_, f32[2048,128]{1,0:T(8,128)} %get-tuple-element.11.refs_2_.refs_4_, bf16[128,2048]{1,0:T(8,128)(2,1)S(1)} %copy-done.3, ...), custom_call_target="tpu_custom_call" | custom-call | flops 20000000000 | bytes 60000000 | tf_op jit(solution)/shard_map/opening/pallas_call | solution.py:458
  44.3 0.0 copy-start.1
  44.3 1.0 copy-done.1
  45.3 0.0 copy-start.2
  45.3 1.0 copy-done.2
  46.3 19.5 %all-gather.2.cloned.1.call-done.m_ref = f32[1024,640]{1,0:T(8,128)} async-done(((f32[128,640]{1,0:T(8,128)}), f32[1024,640]{1,0:T(8,128)}) %all-gather.2.cloned.1.call-update) | async-done | bytes 2621456 | tf_op jit(solution)/shard_map/all_gather | solution.py:437
  65.8 0.0 copy-start
  65.8 1.7 %copy-done = f32[1024,640]{1,0:T(8,128)S(1)} copy-done((f32[1024,640]{1,0:T(8,128)S(1)}, f32[1024,640]{1,0:T(8,128)}, u32[]{:S(2)}) %copy-start) | copy-done | bytes 2621464
  67.5 0.0 copy-start.4
  67.5 0.0 copy-start.5
  67.5 4.9 %poly.1.refs_10_ = bf16[256,1024]{1,0:T(8,128)(2,1)S(1)} custom-call(f32[1024,640]{1,0:T(8,128)S(1)} %copy-done), custom_call_target="tpu_custom_call" | custom-call | tf_op jit(solution)/shard_map/poly/pallas_call | solution.py:160
  72.4 0.0 copy-done.4
  72.4 0.0 copy-done.5
  72.4 77.8 %cycles.1 = (f32[2048,128]{1,0:T(8,128)S(1)}, f32[2048,128]{1,0:T(8,128)S(1)}) custom-call(f32[2048,128]{1,0:T(8,128)} %copy-done.1, f32[2048,128]{1,0:T(8,128)} %copy-done.2, f32[128,128]{1,0:T(8,128)S(1)} %get-tuple-element.15.refs_2_, bf16[4096,256]{1,0:T(8,128)(2,1)} %get-tuple-element.10.refs_1_.refs_3_, f32[2048,128]{1,0:T(8,128)} %get-tuple-element.11.refs_2_.refs_4_, ...), custom_call_target="tpu_custom_call" | custom-call | tf_op jit(solution)/shard_map/cycles/pallas_call | solution.py:469
  150.3 1.0 copy.11
  151.2 1.0 copy.12
Async XLA Ops:
  7.2 58.6 %all-gather.2.cloned.1.call-start = ((), (), s32[]{:S(2)}) async-start(), calls=%async_computation | async-start | bytes 2949120 | tf_op jit(solution)/shard_map/all_gather | solution.py:437
  9.0 14.4 %copy-start.6 = (s32[64]{0:T(128)S(1)}, s32[64]{0:T(128)}, u32[]{:S(2)}) copy-start(s32[64]{0:T(128)} %refs_8_.1) | copy-start | bytes 772
  9.0 14.4 %copy-start.7 = (s32[64]{0:T(128)S(1)}, s32[64]{0:T(128)}, u32[]{:S(2)}) copy-start(s32[64]{0:T(128)} %refs_9_.1) | copy-start | bytes 772
  9.0 14.4 %copy-start.8 = (f32[2048,128]{1,0:T(8,128)S(1)}, f32[2048,128]{1,0:T(8,128)}, u32[]{:S(2)}) copy-start(f32[2048,128]{1,0:T(8,128)} %refs_0_.1) | copy-start | bytes 3145732
  23.4 1.0 copy-start.3
  44.3 1.0 copy-start.1
  45.3 1.0 copy-start.2
  65.8 1.7 %copy-start = (f32[1024,640]{1,0:T(8,128)S(1)}, f32[1024,640]{1,0:T(8,128)}, u32[]{:S(2)}) copy-start(f32[1024,640]{1,0:T(8,128)} %all-gather.2.cloned.1.call-done.m_ref) | copy-start | bytes 7864324
  67.5 4.9 %copy-start.4 = (bf16[128,2048]{1,0:T(8,128)(2,1)S(1)}, bf16[128,2048]{1,0:T(8,128)(2,1)}, u32[]{:S(2)}) copy-start(bf16[128,2048]{1,0:T(8,128)(2,1)} %get-tuple-element.12.refs_3_.refs_6_) | copy-start | bytes 1572868
  67.5 4.9 %copy-start.5 = (bf16[2048,128]{1,0:T(8,128)(2,1)S(1)}, bf16[2048,128]{1,0:T(8,128)(2,1)}, u32[]{:S(2)}) copy-start(bf16[2048,128]{1,0:T(8,128)(2,1)} %get-tuple-element.17.refs_7_) | copy-start | bytes 1572868
Sparse Core Ops, SparseCore 0:
  10.2 55.5 all-gather.1
where the time goes:
time: 160 us; the launch traced here: 159 us
  Pallas kernels  117 us (73%)
  waiting for transfers between devices  19.5 us (12%)
  between operations  14.1 us (9%)
  local copies, waits for them, and re-layouts  6.73 us (4%)
  other arithmetic  1.78 us (1%)
    pallas_call x1, Pallas kernels, body(): pl.pallas_call(functools.partial(main_kernel, False, n_grp, n_sub), in_sp...  77.8 us
    pallas_call x1, Pallas kernels, body(): pl.pallas_call(functools.partial(main_kernel, True, n_grp, n_sub), in_spe...  19.8 us
    all_gather x1, waiting for transfers between devices, body(): matrix = lax.all_gather(slab, 'sub', axis=0, tiled=True)  19.5 us
    pallas_call x1, Pallas kernels, run_setup(): pl.pallas_call(setup_kernel, grid=(blocks,), in_specs=[pl.BlockSpec((entr...  14.3 us
    unnamed x20, local copies, waits for them, and re-layouts  6.73 us
    pallas_call x1, Pallas kernels, run_poly(): pl.pallas_call(poly_kernel, in_specs=[vmem], out_specs=vmem, out_shape=ja...  4.9 us
  transfers between devices with their start and end apart: 1, of which 1 were waited for; matrix products, arithmetic and copies ran while one was open for 0% of the time, Pallas kernels for 21%

commit v1 on v0

v1 whole, which is shorter than its diff:
```python
import functools

import jax
import jax.numpy as jnp
from jax import lax
from jax.experimental import pallas as pl
from jax.experimental.pallas import tpu as pltpu
from jax.sharding import PartitionSpec as P

CHEB_COARSE = 6
CYCLES = 2
ROUNDS = 4
CHUNKS = 2

THETA = 1.0
DELTA = 0.7
OMEGA = 0.6
RHO0 = DELTA / THETA
RHO1 = 1.0 / (2.0 * THETA / DELTA - RHO0)
C1 = RHO1 * RHO0
C2 = 2.0 * RHO1 / DELTA
MESH = pl.DeviceIdType.MESH
f32 = jnp.float32
bf16 = jnp.bfloat16


def split(x):
    hi = x.astype(bf16)
    lo = (x - hi.astype(f32)).astype(bf16)
    return hi, lo


def split_lanes(x):
    hi, lo = split(x)
    return jnp.concatenate([hi, lo], axis=1)


def iota(shape, dim):
    return lax.broadcasted_iota(jnp.int32, shape, dim)


def dot(a, b):
    return jnp.dot(a, b, preferred_element_type=f32)


def quads(product, rows, width):
    return product[:rows, :width] + (product[:rows, width:] + product[rows:, :width])


def aligned(start, size):
    return pl.ds(pl.multiple_of(start, size), size)


def band_tile(fv_ref, col_ref, b, block):
    groups = (fv_ref.shape[0] - 1) // 8
    sl = aligned(b * block, block)
    rows = iota((8, block), 1) + b * block
    cols, vals, firsts = [], [], []
    for i in range(groups):
        cols.append(col_ref[1 + 8 * i : 9 + 8 * i, sl] - rows)
        vals.append(fv_ref[1 + 8 * i : 9 + 8 * i, sl])
    last = jnp.zeros((8, block), f32)
    for i in range(groups):
        last = last + jnp.where(cols[i] == block, vals[i], 0.0)
    last = jnp.sum(last, axis=0, keepdims=True)
    for j in range(groups):
        total = vals[j]
        for i in range(j + 1, groups):
            total = total + jnp.where(cols[i] == cols[j], vals[i], 0.0)
        firsts.append(total)
    high_count = block // 8
    places = [iota((8, block), 0) + 8 * h for h in range(high_count)]
    sums = [jnp.zeros((8, block), f32)] * high_count
    for s in range(8):
        chains = [jnp.zeros((8, block), f32)] * high_count
        for i in reversed(range(groups)):
            col = jnp.broadcast_to(cols[i][s : s + 1, :], (8, block))
            val = jnp.broadcast_to(firsts[i][s : s + 1, :], (8, block))
            chains = [jnp.where(col == places[h], val, chains[h]) for h in range(high_count)]
        sums = [sums[h] + chains[h] for h in range(high_count)]
    by_offset = jnp.concatenate(sums, axis=0).T
    skewed = pltpu.roll(by_offset, 0, 1, stride=1, stride_axis=0)
    lane = iota((block, block), 1)
    sub = iota((block, block), 0)
    low = jnp.where(lane >= sub, skewed, 0.0)
    high = jnp.where(lane < sub, skewed, jnp.where(lane == sub, last, 0.0))
    return low, high


def kernel(n_grp, n_sub, *refs):
    (rhs_ref, fv_ref, col_ref, agg_ref, lo_ref, hi_ref, own_ref,
     sol_ref, res_ref,
     a2, dinv_ref, diag_ref, oh_ref, oht_ref, g_ref, sa, dinv_s,
     xs, ext_v, ext_w, s2, y_mid,
     send, recv, far, r_send, r_recv, r2,
     send_sem, recv_sem, far_send_sem, far_recv_sem, r_send_sem, r_recv_sem,
     slabs, slab_send_sem, slab_recv_sem, m_hi, m_lo, pd, pz, px, pair2, m2,
     csend, whole, csend_sem, crecv_sem) = refs
    rows_dev, width = rhs_ref.shape
    ghost = lo_ref.shape[1]
    block = 2 * ghost
    blocks = rows_dev // block
    agg, coarse = own_ref.shape
    parts = coarse // agg
    kept = slabs.shape[1]
    grp = lax.axis_index("grp")
    me = lax.axis_index("sub")
    total = n_grp * n_sub
    part = grp * n_sub + me
    ones = functools.partial(jnp.asarray, dtype=jnp.int32)

    def device(p):
        return lax.div(p, n_sub), lax.rem(p, n_sub)

    has = {d: jnp.logical_and(part + d >= 0, part + d < total) for d in (1, -1, 2, -2)}

    barrier = pltpu.get_barrier_semaphore()
    for j in range(1, n_sub):
        pl.semaphore_signal(barrier, inc=1, device_id=(grp, lax.rem(me + j, n_sub)), device_id_type=MESH)
    greeted = n_sub - 1
    for d in (1, -1, 2, -2):
        outside = jnp.logical_or(me + d < 0, me + d >= n_sub)
        across = jnp.logical_and(has[d], outside)

        @pl.when(across)
        def _():
            pl.semaphore_signal(barrier, inc=1, device_id=device(part + d), device_id_type=MESH)

        greeted = greeted + across.astype(jnp.int32)

    mine = aligned(me * agg, agg)
    for k in range(kept // agg):
        slabs[mine, k * agg : (k + 1) * agg] = own_ref[:, aligned(lax.rem(me + k, n_sub) * agg, agg)]
    pl.semaphore_wait(barrier, greeted)

    line = n_sub // 2
    pos = lax.div(me, 2)
    odd = lax.rem(me, 2)
    partner = me + 1 - 2 * odd
    chunk = agg // CHUNKS
    RIGHT, LEFT, ACROSS = 0, 1, 2

    def slab_copy(origin, c, way):
        peer = (me + 2, me - 2, partner)[way]
        at = pl.ds(pl.multiple_of(origin * agg + c * chunk, chunk), chunk)
        return pltpu.make_async_remote_copy(
            src_ref=slabs.at[at], dst_ref=slabs.at[at],
            send_sem=slab_send_sem.at[way, lax.div(origin, 2), c],
            recv_sem=slab_recv_sem.at[way, lax.div(origin, 2), c],
            device_id=(grp, peer), device_id_type=MESH,
        )

    def slab_open():
        for c in range(CHUNKS):
            @pl.when(pos + 1 < line)
            def _():
                slab_copy(me, c, RIGHT).start()

            @pl.when(pos > 0)
            def _():
                slab_copy(me, c, LEFT).start()

            slab_copy(me, c, ACROSS).start()

    def slab_pass(event):
        step = 1 + lax.div(event, CHUNKS)
        c = lax.rem(event, CHUNKS)

        @pl.when(pos - step >= 0)
        def _():
            origin = me - 2 * step
            slab_copy(origin, c, RIGHT).wait_recv()

            @pl.when(pos + 1 < line)
            def _():
                slab_copy(origin, c, RIGHT).start()

            slab_copy(origin, c, ACROSS).start()

        @pl.when(pos + step < line)
        def _():
            origin = me + 2 * step
            slab_copy(origin, c, LEFT).wait_recv()

            @pl.when(pos > 0)
            def _():
                slab_copy(origin, c, LEFT).start()

            slab_copy(origin, c, ACROSS).start()

    def slab_close():
        def one(i, carry):
            q = lax.div(i, CHUNKS)
            c = lax.rem(i, CHUNKS)
            slab_copy(2 * q + 1 - odd, c, ACROSS).wait_recv()
            origin = 2 * q + odd
            slab_copy(origin, c, ACROSS).wait_send()

            @pl.when(jnp.logical_and(q <= pos, pos + 1 < line))
            def _():
                slab_copy(origin, c, RIGHT).wait_send()

            @pl.when(jnp.logical_and(q >= pos, pos > 0))
            def _():
                slab_copy(origin, c, LEFT).wait_send()

            return carry

        lax.fori_loop(0, line * CHUNKS, one, 0)

    events = (line - 1) * CHUNKS
    first_event_block = 4
    in_setup = min(events, blocks - first_event_block)
    slab_open()

    for d, slot in ((-1, 0), (1, 1)):
        @pl.when(jnp.logical_not(has[d]))
        def _():
            recv[:, slot] = jnp.zeros((recv.shape[0],) + recv.shape[2:], f32)
            r_recv[slot] = jnp.zeros(r_recv.shape[1:], f32)

    for d, slot in ((-2, 0), (2, 1)):
        @pl.when(jnp.logical_not(has[d]))
        def _():
            far[:, slot] = jnp.zeros((far.shape[0],) + far.shape[2:], f32)

    for ext in (ext_v, ext_w):
        ext[:ghost, :] = jnp.zeros((ghost, 2 * width), bf16)
        ext[ghost + rows_dev :, :] = jnp.zeros((ghost, 2 * width), bf16)
    sent_row = jnp.concatenate([hi_ref[...], lo_ref[...]], axis=1).astype(f32)
    sent = jnp.broadcast_to(sent_row, (2 * ghost, 2 * ghost)).T.astype(jnp.int32)
    lane = iota((2 * ghost, block), 1)
    for j in range(blocks + 1):
        g_ref[: 2 * ghost, j * block : (j + 1) * block] = (sent + (ghost - j * block) == lane).astype(f32).astype(bf16)
    dinv_s[...] = jnp.zeros_like(dinv_s)
    sa[:, :block] = jnp.zeros((2 * ghost, block), f32)

    def setup(b, carry):
        sl = aligned(b * block, block)
        low, high = band_tile(fv_ref, col_ref, b, block)
        diag = jnp.broadcast_to(fv_ref[0:1, sl], (block, block)).T
        dinv = 1.0 / diag
        diag_ref[sl, :] = diag
        dinv_ref[sl, :] = dinv
        low_hi, low_lo = split(low)
        high_hi, high_lo = split(high)
        hi = jnp.concatenate([low_hi, high_hi], axis=1)
        lo = jnp.concatenate([low_lo, high_lo], axis=1)
        a2[aligned(b * 2 * block, block), :] = hi
        a2[aligned(b * 2 * block + block, block), :] = lo
        onehot = (iota((agg, block), 0) == agg_ref[:, sl]).astype(f32)
        oht_ref[:, sl] = onehot.astype(bf16)
        oh_ref[sl, :] = onehot.T.astype(bf16)
        picked = (sent - b * block == lane).astype(f32).astype(bf16)
        part_sa = dot(picked, hi) + dot(picked, lo)
        sa[:, sl] = sa[:, sl] + part_sa[:, :block]
        sa[:, aligned((b + 1) * block, block)] = part_sa[:, block:]
        both = dot(picked, split_lanes(dinv))
        dinv_s[...] += both[:, :block] + both[:, block:]
        rhs = rhs_ref[sl, :]
        res_ref[sl, :] = rhs
        sol_ref[sl, :] = jnp.zeros_like(rhs)
        v = dinv * rhs
        xs[sl, :] = v
        ext_v[pl.ds(pl.multiple_of(ghost + b * block, ghost), block), :] = split_lanes(v)

        @pl.when(jnp.logical_and(b >= first_event_block, b < first_event_block + in_setup))
        def _():
            slab_pass(b - first_event_block)

        return carry

    lax.fori_loop(0, blocks, setup, 0)
    for j in range(blocks + 1):
        at = slice(j * block, (j + 1) * block)
        scaled = sa[:, at] * dinv_s[...]
        g_ref[2 * ghost : 4 * ghost, at], g_ref[4 * ghost :, at] = split(scaled)
        if j == 0:
            below = scaled
    response = jnp.where(lane < ghost, below, scaled)
    r_send[0] = response[:ghost]
    r_send[1] = response[ghost:]

    def r_copy(way):
        d = (1, -1)[way]
        return pltpu.make_async_remote_copy(
            src_ref=r_send.at[way], dst_ref=r_recv.at[way],
            send_sem=r_send_sem.at[way], recv_sem=r_recv_sem.at[way],
            device_id=device(part + d), device_id_type=MESH,
        )

    def near_copy(ex, way, count):
        d = (1, -1)[way]
        return pltpu.make_async_remote_copy(
            src_ref=send.at[ex, way, pl.ds(0, count)], dst_ref=recv.at[ex, way, pl.ds(0, count)],
            send_sem=send_sem.at[ex, way], recv_sem=recv_sem.at[ex, way],
            device_id=device(part + d), device_id_type=MESH,
        )

    def far_copy(ex, way):
        d = (2, -2)[way]
        return pltpu.make_async_remote_copy(
            src_ref=send.at[ex, way, pl.ds(0, ghost)], dst_ref=far.at[ex, way],
            send_sem=far_send_sem.at[ex, way], recv_sem=far_recv_sem.at[ex, way],
            device_id=device(part + d), device_id_type=MESH,
        )

    def mid_product(double):
        high = 6 * ghost if double else 2 * ghost
        inner = slice(2 * block, (blocks - 1) * block)
        y_mid[:high] = dot(g_ref[:high, inner], ext_v[inner, :])

    def depart(ex, double, alpha, beta):
        high = 6 * ghost if double else 2 * ghost
        y = y_mid[:high]
        for ends in (slice(0, 2 * block), slice((blocks - 1) * block, (blocks + 1) * block)):
            y = y + dot(g_ref[:high, ends], ext_v[ends, :])
        now = y[: 2 * ghost, :width] + y[: 2 * ghost, width:]
        for way in range(2):
            send[ex, way, :ghost] = now[way * ghost : (way + 1) * ghost]
        if double:
            later = alpha * now - beta * quads(y[2 * ghost :], 2 * ghost, width)
            for way in range(2):
                send[ex, way, ghost:] = later[way * ghost : (way + 1) * ghost]
        for way, d in ((0, 1), (1, -1)):
            @pl.when(has[d])
            def _():
                near_copy(ex, way, 2 * ghost if double else ghost).start()
        if double:
            for way, d in ((0, 2), (1, -2)):
                @pl.when(has[d])
                def _():
                    far_copy(ex, way).start()

    def arrive(ex, double):
        count = 2 * ghost if double else ghost
        for way, d in ((0, 1), (1, -1)):
            @pl.when(has[-d])
            def _():
                near_copy(ex, way, count).wait_recv()

            @pl.when(has[d])
            def _():
                near_copy(ex, way, count).wait_send()
        if double:
            for way, d in ((0, 2), (1, -2)):
                @pl.when(has[-d])
                def _():
                    far_copy(ex, way).wait_recv()

                @pl.when(has[d])
                def _():
                    far_copy(ex, way).wait_send()

    def local_apply(ext, fn):
        def go(b, carry):
            a = a2[aligned(b * 2 * block, 2 * block), :]
            x = ext[pl.ds(pl.multiple_of(b * block, block), 2 * block), :]
            fn(b, aligned(b * block, block), quads(dot(a, x), block, width))
            return carry

        lax.fori_loop(0, blocks, go, 0, unroll=4)

    def store_ext(ext, b, x):
        ext[pl.ds(pl.multiple_of(ghost + b * block, ghost), block), :] = split_lanes(x)

    last_tile = (blocks - 1) * 2 * block
    below_rows = slice(0, ghost)
    above_rows = slice(rows_dev - ghost, rows_dev)

    def ghost_terms(ex):
        nothing = jnp.zeros((ghost, 2 * width), bf16)
        a_below = jnp.concatenate([a2[:ghost, :block], a2[block : block + ghost, :block]], axis=0)
        a_above = jnp.concatenate(
            [a2[last_tile + ghost : last_tile + block, block:], a2[last_tile + block + ghost : last_tile + 2 * block, block:]],
            axis=0,
        )
        from_below = jnp.concatenate([split_lanes(recv[ex, 0, :ghost]), nothing], axis=0)
        from_above = jnp.concatenate([nothing, split_lanes(recv[ex, 1, :ghost])], axis=0)
        return quads(dot(a_below, from_below), ghost, width), quads(dot(a_above, from_above), ghost, width)

    def pair(ex, te):
        alpha, beta = (1.0 - OMEGA, OMEGA) if te else (C1, C2)
        gamma = OMEGA if te else C2 - 1.0
        depart(ex, True, alpha, beta)

        def first(b, sl, off):
            v = xs[sl, :]
            w = alpha * v - beta * (dinv_ref[sl, :] * off)
            store_ext(ext_w, b, w)
            r = res_ref[sl, :]
            if te:
                res_ref[sl, :] = r - alpha * (diag_ref[sl, :] * v) + gamma * off
                sol_ref[sl, :] += w
            else:
                res_ref[sl, :] = gamma * off - alpha * r
                sol_ref[sl, :] += v + w

        local_apply(ext_v, first)

        def second(b, sl, off):
            r = res_ref[sl, :] - off
            res_ref[sl, :] = r
            v = dinv_ref[sl, :] * r
            xs[sl, :] = v
            store_ext(ext_v, b, v)

        local_apply(ext_w, second)
        mid_product(True)
        arrive(ex, True)
        off_below, off_above = ghost_terms(ex)
        dw_below = -beta * (dinv_ref[below_rows, :] * off_below)
        dw_above = -beta * (dinv_ref[above_rows, :] * off_above)
        seen_below = jnp.concatenate([split_lanes(far[ex, 0]), split_lanes(send[ex, 1, :ghost])], axis=0)
        seen_above = jnp.concatenate([split_lanes(send[ex, 0, :ghost]), split_lanes(far[ex, 1])], axis=0)
        next_below = recv[ex, 0, ghost:] - beta * quads(dot(r2[0], seen_below), ghost, width)
        next_above = recv[ex, 1, ghost:] - beta * quads(dot(r2[1], seen_above), ghost, width)
        add_below = jnp.concatenate([split_lanes(next_below), split_lanes(dw_below)], axis=0)
        add_above = jnp.concatenate([split_lanes(dw_above), split_lanes(next_above)], axis=0)
        more_below = quads(dot(a2[: 2 * block, :block], add_below), block, width)
        more_above = quads(dot(a2[last_tile:, block:], add_above), block, width)
        zero = jnp.zeros((ghost, width), f32)
        dr_below = jnp.concatenate([gamma * off_below, zero], axis=0) - more_below
        dr_above = jnp.concatenate([zero, gamma * off_above], axis=0) - more_above
        sol_ref[below_rows, :] += dw_below
        sol_ref[above_rows, :] += dw_above
        for b, dr in ((0, dr_below), (blocks - 1, dr_above)):
            sl = slice(b * block, (b + 1) * block)
            r = res_ref[sl, :] + dr
            res_ref[sl, :] = r
            v = dinv_ref[sl, :] * r
            xs[sl, :] = v
            ext_v[ghost + b * block : ghost + (b + 1) * block, :] = split_lanes(v)

    def restricted(ex):
        depart(ex, False, 0.0, 0.0)

        def restrict(b, sl, off):
            s2[sl, :] = split_lanes((1.0 - OMEGA) * res_ref[sl, :] - OMEGA * off)

        local_apply(ext_v, restrict)
        both = dot(oht_ref[...], s2[...])
        arrive(ex, False)
        off_below, off_above = ghost_terms(ex)
        nothing = jnp.zeros((ghost, 2 * width), bf16)
        ds_below = jnp.concatenate([split_lanes(-OMEGA * off_below), nothing], axis=0)
        ds_above = jnp.concatenate([nothing, split_lanes(-OMEGA * off_above)], axis=0)
        both = both + dot(oht_ref[:, :block], ds_below) + dot(oht_ref[:, rows_dev - block :], ds_above)
        return both[:, :width] + both[:, width:]

    def polynomial():
        half = parts // 2
        eye = iota((agg, agg), 0) == iota((agg, agg), 1)
        cinv = []
        for j in range(parts):
            sl = slice(j * agg, (j + 1) * agg)
            cinv.append(1.0 / jnp.sum(jnp.where(eye, slabs[sl, :agg], 0.0), axis=0, keepdims=True))
            for k in range(half + 1):
                other = (j + k) % parts
                so = slice(other * agg, (other + 1) * agg)
                tile = slabs[sl, k * agg : (k + 1) * agg]
                m_hi[sl, so], m_lo[sl, so] = split(tile)
                if 0 < k and 2 * k < parts:
                    m_hi[so, sl], m_lo[so, sl] = split(tile.T)
        for j in range(parts):
            sl = slice(j * agg, (j + 1) * agg)
            start = jnp.where(jnp.logical_and(eye, me == j), cinv[j], 0.0)
            pd[:, sl] = start
            pz[:, sl] = start
            px[:, sl] = start
        rho_old = RHO0
        for turn in range(1, CHEB_COARSE):
            rho_new = 1.0 / (2.0 * THETA / DELTA - rho_old)
            hi, lo = split(pd[...])
            pair2[:agg, :] = hi
            pair2[agg:, :] = lo
            for j in range(parts // 2):
                sl = slice(2 * j * agg, (2 * j + 2) * agg)
                both = dot(pair2[...], m_hi[:, sl])
                low = dot(pair2[:agg, :], m_lo[:, sl])
                scale = jnp.concatenate([cinv[2 * j], cinv[2 * j + 1]], axis=1)
                z = pz[:, sl] - (both[:agg] + (both[agg:] + low)) * scale
                d = rho_new * rho_old * pd[:, sl] + (2.0 * rho_new / DELTA) * z
                pz[:, sl] = z
                pd[:, sl] = d
                px[:, sl] += d
            rho_old = rho_new
        hi, lo = split(px[...])
        m2[:agg, :] = hi
        m2[agg:, :] = lo

    def gather(step):
        half = n_sub // 2

        def block_copy(source, origin, slot, peer):
            return pltpu.make_async_remote_copy(
                src_ref=source, dst_ref=whole.at[step, aligned(origin * agg, agg)],
                send_sem=csend_sem.at[step, slot], recv_sem=crecv_sem.at[step, slot],
                device_id=(grp, peer), device_id_type=MESH,
            )

        copies = [block_copy(csend.at[step], me, 0, partner)]
        for j in range(1, half):
            copies.append(block_copy(csend.at[step], me, j, lax.rem(me + 2 * j, n_sub)))
        for copy in copies:
            copy.start()
        whole[step, mine, :] = csend[step]
        passed = []
        for j in range(1, half):
            copies[j].wait_recv()
            origin = lax.rem(me + n_sub - 2 * j, n_sub)
            copy = block_copy(whole.at[step, aligned(origin * agg, agg)], origin, half + j, partner)
            copy.start()
            passed.append(copy)
        copies[0].wait_recv()
        for copy in passed:
            copy.wait_recv()
        for copy in copies + passed:
            copy.wait_send()

    for way, d in ((0, 1), (1, -1)):
        @pl.when(has[d])
        def _():
            r_copy(way).start()
    mid_product(True)

    def cycle_body(cycle, carry):
        ex = cycle * ROUNDS

        @pl.when(cycle == 0)
        def _():
            for way, d in ((0, 1), (1, -1)):
                @pl.when(has[-d])
                def _():
                    r_copy(way).wait_recv()

                @pl.when(has[d])
                def _():
                    r_copy(way).wait_send()

                hi, lo = split(r_recv[way])
                r2[way, :ghost] = hi
                r2[way, ghost:] = lo

        pair(ex, False)
        csend[cycle] = restricted(ex + 1)

        @pl.when(cycle == 0)
        def _():
            def rest(event, c):
                slab_pass(event)
                return c

            lax.fori_loop(in_setup, events, rest, 0)
            slab_close()
            polynomial()

        gather(cycle)
        corr = split_lanes(quads(dot(m2[...], split_lanes(whole[cycle])), agg, width))

        def spread(b, c):
            sl = aligned(b * block, block)
            both = dot(oh_ref[sl, :], corr)
            t = both[:, :width] + both[:, width:]
            xs[sl, :] = t
            store_ext(ext_v, b, t)
            return c

        lax.fori_loop(0, blocks, spread, 0, unroll=4)
        mid_product(True)
        pair(ex + 2, True)
        pair(ex + 3, False)
        return carry

    lax.fori_loop(0, CYCLES, cycle_body, 0)


def body(n_grp, n_sub, right_side, fine_values, columns, agg_map, send_lo, send_hi, coarse_matrix):
    rows, width = right_side.shape
    ghost = send_lo.shape[0]
    block = 2 * ghost
    own = coarse_matrix[0]
    agg, coarse = own.shape
    kept = (coarse // agg // 2 + 1) * agg
    ext_rows = rows + block
    exchanges = CYCLES * ROUNDS
    vmem = pl.BlockSpec(memory_space=pltpu.VMEM)
    field = jax.ShapeDtypeStruct((rows, width), f32)
    dma = pltpu.SemaphoreType.DMA
    return pl.pallas_call(
        functools.partial(kernel, n_grp, n_sub),
        in_specs=[vmem] * 7,
        out_specs=[vmem] * 2,
        out_shape=[field] * 2,
        scratch_shapes=[
            pltpu.VMEM((2 * rows, 2 * block), bf16),
            pltpu.VMEM((rows, block), f32),
            pltpu.VMEM((rows, block), f32),
            pltpu.VMEM((rows, agg), bf16),
            pltpu.VMEM((agg, rows), bf16),
            pltpu.VMEM((6 * ghost, ext_rows), bf16),
            pltpu.VMEM((2 * ghost, ext_rows), f32),
            pltpu.VMEM((2 * ghost, block), f32),
            pltpu.VMEM((rows, width), f32),
            pltpu.VMEM((ext_rows, 2 * width), bf16),
            pltpu.VMEM((ext_rows, 2 * width), bf16),
            pltpu.VMEM((rows, 2 * width), bf16),
            pltpu.VMEM((6 * ghost, 2 * width), f32),
            pltpu.VMEM((exchanges, 2, 2 * ghost, width), f32),
            pltpu.VMEM((exchanges, 2, 2 * ghost, width), f32),
            pltpu.VMEM((exchanges, 2, ghost, width), f32),
            pltpu.VMEM((2, ghost, 2 * ghost), f32),
            pltpu.VMEM((2, ghost, 2 * ghost), f32),
            pltpu.VMEM((2, 2 * ghost, 2 * ghost), bf16),
            dma((exchanges, 2)),
            dma((exchanges, 2)),
            dma((exchanges, 2)),
            dma((exchanges, 2)),
            dma((2,)),
            dma((2,)),
            pltpu.VMEM((coarse, kept), f32),
            dma((3, n_sub // 2, CHUNKS)),
            dma((3, n_sub // 2, CHUNKS)),
            pltpu.VMEM((coarse, coarse), bf16),
            pltpu.VMEM((coarse, coarse), bf16),
            pltpu.VMEM((agg, coarse), f32),
            pltpu.VMEM((agg, coarse), f32),
            pltpu.VMEM((agg, coarse), f32),
            pltpu.VMEM((2 * agg, coarse), bf16),
            pltpu.VMEM((2 * agg, coarse), bf16),
            pltpu.VMEM((CYCLES, agg, width), f32),
            pltpu.VMEM((CYCLES, coarse, width), f32),
            dma((CYCLES, n_sub)),
            dma((CYCLES, n_sub)),
        ],
        compiler_params=pltpu.CompilerParams(
            collective_id=0, has_side_effects=True, vmem_limit_bytes=60 * 1024 * 1024
        ),
        name="cycles",
    )(
        right_side, fine_values, columns, agg_map.reshape(1, rows),
        send_lo.reshape(1, ghost), send_hi.reshape(1, ghost), own,
    )


def solution(mesh):
    placed = (
        P(("grp", "sub"), None),
        P(None, ("grp", "sub")),
        P(None, ("grp", "sub")),
        P(("grp", "sub")),
        P(("grp", "sub")),
        P(("grp", "sub")),
        P("grp", "sub", None),
    )
    return jax.shard_map(
        functools.partial(body, mesh.shape["grp"], mesh.shape["sub"]),
        mesh=mesh,
        in_specs=placed,
        out_specs=(P(("grp", "sub"), None), P(("grp", "sub"), None)),
        check_vma=False,
    )
```

time: 160 us -> 116 us (0.72)
  waiting for transfers between devices: 19.5 us -> 0 us
  between operations: 14.1 us -> 0.65 us
  Pallas kernels: 117 us -> 112 us
  local copies, waits for them, and re-layouts: 6.73 us -> 3.32 us
  other arithmetic: 1.78 us -> 0 us
    all_gather x1 -> x0, waiting for transfers between devices: 19.5 us -> none  [body(): matrix = lax.all_gather(slab, 'sub', axis=0, tiled=True)]
    pallas_call x4 -> x1, Pallas kernels: 117 us -> 112 us  [body(): pl.pallas_call(functools.partial(kernel, n_grp, n_sub), in_specs=[vmem] *...]
    unnamed x20 -> x4, local copies, waits for them, and re-layouts: 6.73 us -> 3.32 us
    concatenate x1 -> x0, other arithmetic: 1.78 us -> none  [body(): jnp.concatenate([own, own], 1)]
  transfers between devices with their start and end apart: 1 -> 0, of which waited for: 1 -> 0; matrix products, arithmetic and copies ran while one was open for 0% -> 0% of each run, Pallas kernels for 21% -> 0%
where the time goes in v1:
time: 116 us
  Pallas kernels  112 us (97%)
  local copies, waits for them, and re-layouts  3.32 us (3%)
    pallas_call x1, Pallas kernels, body(): pl.pallas_call(functools.partial(kernel, n_grp, n_sub), in_specs=[vmem] *...  112 us
    unnamed x4, local copies, waits for them, and re-layouts  3.32 us

profile of v1, /device:TPU:1, one launch (start us, length us, event | category | flops | bytes accessed | tf_op | source)
XLA Modules:
  0.0 115.9 jit_solution(2663632312388692130)
XLA Ops:
  0.6 111.9 %cycles.1 = (f32[2048,128]{1,0:T(8,128)}, f32[2048,128]{1,0:T(8,128)}) custom-call(f32[2048,128]{1,0:T(8,128)} %refs_0_.1, f32[81,2048]{1,0:T(8,128)} %refs_1_.1, s32[81,2048]{1,0:T(8,128)} %refs_2_.1, s32[1,2048]{1,0:T(1,128)} %bitcast.5, s32[1,64]{1,0:T(1,128)} %bitcast.6, s32[1,64]{1,0:T(1,128)} %bitcast.7, f32[128,1024]{1,0:T(8,128)} %bitcast.4), custom_call_target="tpu_custom_call" | custom-call | tf_op jit(solution)/shard_map/cycles/pallas_call | solution.py:590
  112.6 0.0 copy-start
  112.6 2.4 %copy.11 = f32[2048,128]{1,0:T(8,128)} copy(f32[2048,128]{1,0:T(8,128)} %get-tuple-element.4) | data formatting | bytes 2097152
  114.9 0.0 copy-done
  114.9 1.0 copy.12
Async XLA Ops:
  112.6 2.4 %copy-start = (f32[2048,128]{1,0:T(8,128)S(1)}, f32[2048,128]{1,0:T(8,128)}, u32[]{:S(2)}) copy-start(f32[2048,128]{1,0:T(8,128)} %get-tuple-element.5) | copy-start | bytes 3145732

commit v2 on v1

--- a/solution.py
+++ b/solution.py
@@ -10,7 +10,9 @@
 CHEB_COARSE = 6
 CYCLES = 2
 ROUNDS = 4
-CHUNKS = 2
+FIRST = 1
+CHUNKS = 4
+PIECES = 2
 
 THETA = 1.0
 DELTA = 0.7
@@ -88,14 +90,19 @@
 
 
 def kernel(n_grp, n_sub, *refs):
-    (rhs_ref, fv_ref, col_ref, agg_ref, lo_ref, hi_ref, own_ref,
-     sol_ref, res_ref,
+    ins = refs[:7]
+    (sol_ref, res_ref,
+     rhs_ref, fv_ref, col_ref, agg_ref, lo_ref, hi_ref, own_ref, in_sem,
      a2, dinv_ref, diag_ref, oh_ref, oht_ref, g_ref, sa, dinv_s,
      xs, ext_v, ext_w, s2, y_mid,
      send, recv, far, r_send, r_recv, r2,
      send_sem, recv_sem, far_send_sem, far_recv_sem, r_send_sem, r_recv_sem,
-     slabs, slab_send_sem, slab_recv_sem, m_hi, m_lo, pd, pz, px, pair2, m2,
-     csend, whole, csend_sem, crecv_sem) = refs
+     slabs, slab_send_sem, slab_recv_sem, cinv_ref, m_hi, m_lo, pd, pz, px, pair2, m2,
+     whole, line_send, line_recv, over_send, over_recv, go_ref) = refs[7:]
+    held = (rhs_ref, fv_ref, col_ref, agg_ref, lo_ref, hi_ref, own_ref)
+    loads = [pltpu.make_async_copy(ins[i], held[i], in_sem.at[i]) for i in range(7)]
+    for i in (6, 1, 2, 4, 5, 0, 3):
+        loads[i].start()
     rows_dev, width = rhs_ref.shape
     ghost = lo_ref.shape[1]
     block = 2 * ghost
@@ -129,88 +136,124 @@
         greeted = greeted + across.astype(jnp.int32)
 
     mine = aligned(me * agg, agg)
+    loads[6].wait()
     for k in range(kept // agg):
         slabs[mine, k * agg : (k + 1) * agg] = own_ref[:, aligned(lax.rem(me + k, n_sub) * agg, agg)]
     pl.semaphore_wait(barrier, greeted)
 
     line = n_sub // 2
-    pos = lax.div(me, 2)
     odd = lax.rem(me, 2)
     partner = me + 1 - 2 * odd
+    place = jnp.where(odd == 1, lax.div(me, 2), n_sub - 1 - lax.div(me, 2))
     chunk = agg // CHUNKS
-    RIGHT, LEFT, ACROSS = 0, 1, 2
-
-    def slab_copy(origin, c, way):
-        peer = (me + 2, me - 2, partner)[way]
-        at = pl.ds(pl.multiple_of(origin * agg + c * chunk, chunk), chunk)
-        return pltpu.make_async_remote_copy(
-            src_ref=slabs.at[at], dst_ref=slabs.at[at],
-            send_sem=slab_send_sem.at[way, lax.div(origin, 2), c],
-            recv_sem=slab_recv_sem.at[way, lax.div(origin, 2), c],
-            device_id=(grp, peer), device_id_type=MESH,
-        )
+    halved = CHUNKS // 2
+    UP, DOWN = range(2)
+
+    def at_place(q):
+        q = lax.rem(q + n_sub, n_sub)
+        return jnp.where(q < line, 2 * q + 1, 2 * (n_sub - 1 - q))
+
+    def origin_of(step, way):
+        return at_place(place - step if way == UP else place + step)
+
+    def slab(origin, step, c, way, act):
+        peer = at_place(place + 1 if way == UP else place - 1)
+
+        def copy(columns):
+            at = pl.ds(pl.multiple_of(origin * agg + c * chunk, chunk), chunk)
+            act(pltpu.make_async_remote_copy(
+                src_ref=slabs.at[at, pl.ds(0, columns)], dst_ref=slabs.at[at, pl.ds(0, columns)],
+                send_sem=slab_send_sem.at[way, step, c], recv_sem=slab_recv_sem.at[way, step, c],
+                device_id=(grp, peer), device_id_type=MESH,
+            ))
+
+        @pl.when(origin < line)
+        def _():
+            copy(kept)
+
+        @pl.when(origin >= line)
+        def _():
+            copy(kept - agg)
+
+    def start(copy):
+        copy.start()
+
+    def wait_send(copy):
+        copy.wait_send()
+
+    def wait_recv(copy):
+        copy.wait_recv()
 
     def slab_open():
-        for c in range(CHUNKS):
-            @pl.when(pos + 1 < line)
+        def one(c, carry):
+            for way in (UP, DOWN):
+                slab(me, 0, c, way, start)
+            return carry
+
+        lax.fori_loop(0, CHUNKS, one, 0)
+
+    events = (line - 1) * CHUNKS + halved
+
+    def slab_passes(first, last):
+        def one(event, carry):
+            step = lax.div(event, CHUNKS)
+            c = lax.rem(event, CHUNKS)
+            for way in (UP, DOWN):
+                at = c if way == UP else lax.rem(c + halved, CHUNKS)
+                origin = origin_of(step + 1, way)
+                slab(origin, step, at, way, wait_recv)
+
+                @pl.when(event + CHUNKS < (line - 1) * CHUNKS + halved)
+                def _():
+                    slab(origin, step + 1, at, way, start)
+
+            return carry
+
+        lax.fori_loop(first, last, one, 0)
+
+    def slab_close():
+        def one(event, carry):
+            step = lax.div(event, CHUNKS)
+            c = lax.rem(event, CHUNKS)
+            for way in (UP, DOWN):
+                slab(origin_of(step, way), step, c if way == UP else lax.rem(c + halved, CHUNKS), way, wait_send)
+            return carry
+
+        lax.fori_loop(0, events, one, 0)
+
+    half = parts // 2
+    eye = iota((agg, agg), 0) == iota((agg, agg), 1)
+
+    def take_slab(j):
+        sl = aligned(j * agg, agg)
+        cinv_ref[:, sl] = 1.0 / jnp.sum(jnp.where(eye, slabs[sl, :agg], 0.0), axis=0, keepdims=True)
+
+        def place_tile(k):
+            so = aligned(lax.rem(j + k, parts) * agg, agg)
+            tile = slabs[sl, k * agg : (k + 1) * agg]
+            m_hi[sl, so], m_lo[sl, so] = split(tile)
+            if k:
+                m_hi[so, sl], m_lo[so, sl] = split(tile.T)
+
+        for k in range(half):
+            place_tile(k)
+
+        @pl.when(j < half)
+        def _():
+            place_tile(half)
+
+    def take_slabs(first, last):
+        def one(step, carry):
+            take_slab(origin_of(step, UP))
+
+            @pl.when(jnp.logical_and(step > 0, step < line))
             def _():
-                slab_copy(me, c, RIGHT).start()
-
-            @pl.when(pos > 0)
-            def _():
-                slab_copy(me, c, LEFT).start()
-
-            slab_copy(me, c, ACROSS).start()
-
-    def slab_pass(event):
-        step = 1 + lax.div(event, CHUNKS)
-        c = lax.rem(event, CHUNKS)
-
-        @pl.when(pos - step >= 0)
-        def _():
-            origin = me - 2 * step
-            slab_copy(origin, c, RIGHT).wait_recv()
-
-            @pl.when(pos + 1 < line)
-            def _():
-                slab_copy(origin, c, RIGHT).start()
-
-            slab_copy(origin, c, ACROSS).start()
-
-        @pl.when(pos + step < line)
-        def _():
-            origin = me + 2 * step
-            slab_copy(origin, c, LEFT).wait_recv()
-
-            @pl.when(pos > 0)
-            def _():
-                slab_copy(origin, c, LEFT).start()
-
-            slab_copy(origin, c, ACROSS).start()
-
-    def slab_close():
-        def one(i, carry):
-            q = lax.div(i, CHUNKS)
-            c = lax.rem(i, CHUNKS)
-            slab_copy(2 * q + 1 - odd, c, ACROSS).wait_recv()
-            origin = 2 * q + odd
-            slab_copy(origin, c, ACROSS).wait_send()
-
-            @pl.when(jnp.logical_and(q <= pos, pos + 1 < line))
-            def _():
-                slab_copy(origin, c, RIGHT).wait_send()
-
-            @pl.when(jnp.logical_and(q >= pos, pos > 0))
-            def _():
-                slab_copy(origin, c, LEFT).wait_send()
+                take_slab(origin_of(step, DOWN))
 
             return carry
 
-        lax.fori_loop(0, line * CHUNKS, one, 0)
-
-    events = (line - 1) * CHUNKS
-    first_event_block = 4
-    in_setup = min(events, blocks - first_event_block)
+        lax.fori_loop(first, last, one, 0)
+
     slab_open()
 
     for d, slot in ((-1, 0), (1, 1)):
@@ -227,36 +270,29 @@
     for ext in (ext_v, ext_w):
         ext[:ghost, :] = jnp.zeros((ghost, 2 * width), bf16)
         ext[ghost + rows_dev :, :] = jnp.zeros((ghost, 2 * width), bf16)
+    for i in (1, 2, 4, 5, 0, 3):
+        loads[i].wait()
     sent_row = jnp.concatenate([hi_ref[...], lo_ref[...]], axis=1).astype(f32)
     sent = jnp.broadcast_to(sent_row, (2 * ghost, 2 * ghost)).T.astype(jnp.int32)
     lane = iota((2 * ghost, block), 1)
     for j in range(blocks + 1):
         g_ref[: 2 * ghost, j * block : (j + 1) * block] = (sent + (ghost - j * block) == lane).astype(f32).astype(bf16)
     dinv_s[...] = jnp.zeros_like(dinv_s)
+    oh_ref[:ghost, :] = jnp.zeros((ghost, agg), bf16)
+    oh_ref[ghost + rows_dev :, :] = jnp.zeros((ghost, agg), bf16)
     sa[:, :block] = jnp.zeros((2 * ghost, block), f32)
 
-    def setup(b, carry):
+    def fine(b):
         sl = aligned(b * block, block)
         low, high = band_tile(fv_ref, col_ref, b, block)
         diag = jnp.broadcast_to(fv_ref[0:1, sl], (block, block)).T
         dinv = 1.0 / diag
         diag_ref[sl, :] = diag
         dinv_ref[sl, :] = dinv
-        low_hi, low_lo = split(low)
-        high_hi, high_lo = split(high)
-        hi = jnp.concatenate([low_hi, high_hi], axis=1)
-        lo = jnp.concatenate([low_lo, high_lo], axis=1)
-        a2[aligned(b * 2 * block, block), :] = hi
-        a2[aligned(b * 2 * block + block, block), :] = lo
-        onehot = (iota((agg, block), 0) == agg_ref[:, sl]).astype(f32)
-        oht_ref[:, sl] = onehot.astype(bf16)
-        oh_ref[sl, :] = onehot.T.astype(bf16)
-        picked = (sent - b * block == lane).astype(f32).astype(bf16)
-        part_sa = dot(picked, hi) + dot(picked, lo)
-        sa[:, sl] = sa[:, sl] + part_sa[:, :block]
-        sa[:, aligned((b + 1) * block, block)] = part_sa[:, block:]
-        both = dot(picked, split_lanes(dinv))
-        dinv_s[...] += both[:, :block] + both[:, block:]
+        for at, tile in ((0, low), (block, high)):
+            hi, lo = split(tile)
+            a2[aligned(b * 2 * block, block), at : at + block] = hi
+            a2[aligned(b * 2 * block + block, block), at : at + block] = lo
         rhs = rhs_ref[sl, :]
         res_ref[sl, :] = rhs
         sol_ref[sl, :] = jnp.zeros_like(rhs)
@@ -264,19 +300,40 @@
         xs[sl, :] = v
         ext_v[pl.ds(pl.multiple_of(ghost + b * block, ghost), block), :] = split_lanes(v)
 
-        @pl.when(jnp.logical_and(b >= first_event_block, b < first_event_block + in_setup))
-        def _():
-            slab_pass(b - first_event_block)
-
+    def setup(i, carry):
+        for u in range(2):
+            fine(2 * i + u)
+        slab_passes(jnp.clip(i - FIRST, 0, events), jnp.clip(i + 1 - FIRST, 0, events))
         return carry
 
-    lax.fori_loop(0, blocks, setup, 0)
+    lax.fori_loop(0, blocks // 2, setup, 0)
+    done = min(blocks // 2 - FIRST, events)
+    ends = [done] + [min(done + n, events) for n in (2, 3, 4, 5)]
+
+    def sent_rows(b, carry):
+        sl = aligned(b * block, block)
+        onehot = (iota((agg, block), 0) == agg_ref[:, sl]).astype(f32)
+        oht_ref[:, sl] = onehot.astype(bf16)
+        oh_ref[pl.ds(pl.multiple_of(ghost + b * block, ghost), block), :] = onehot.T.astype(bf16)
+        picked = (sent - b * block == lane).astype(f32).astype(bf16)
+        both = dot(picked, a2[aligned(b * 2 * block, block), :]) + dot(picked, a2[aligned(b * 2 * block + block, block), :])
+        sa[:, sl] = sa[:, sl] + both[:, :block]
+        sa[:, aligned((b + 1) * block, block)] = both[:, block:]
+        both = dot(picked, split_lanes(dinv_ref[sl, :]))
+        dinv_s[...] += both[:, :block] + both[:, block:]
+        return carry
+
+    lax.fori_loop(0, blocks, sent_rows, 0, unroll=4)
+    slab_passes(ends[0], ends[1])
     for j in range(blocks + 1):
         at = slice(j * block, (j + 1) * block)
         scaled = sa[:, at] * dinv_s[...]
         g_ref[2 * ghost : 4 * ghost, at], g_ref[4 * ghost :, at] = split(scaled)
         if j == 0:
             below = scaled
+    spread_sent = dot(g_ref[...], oh_ref[...])
+    go_ref[: 2 * ghost] = spread_sent[: 2 * ghost].astype(bf16)
+    go_ref[2 * ghost : 4 * ghost], go_ref[4 * ghost :] = split(spread_sent[2 * ghost : 4 * ghost] + spread_sent[4 * ghost :])
     response = jnp.where(lane < ghost, below, scaled)
     r_send[0] = response[:ghost]
     r_send[1] = response[ghost:]
@@ -310,11 +367,14 @@
         inner = slice(2 * block, (blocks - 1) * block)
         y_mid[:high] = dot(g_ref[:high, inner], ext_v[inner, :])
 
-    def depart(ex, double, alpha, beta):
+    def all_sent(double):
         high = 6 * ghost if double else 2 * ghost
         y = y_mid[:high]
-        for ends in (slice(0, 2 * block), slice((blocks - 1) * block, (blocks + 1) * block)):
-            y = y + dot(g_ref[:high, ends], ext_v[ends, :])
+        for rim in (slice(0, 2 * block), slice((blocks - 1) * block, (blocks + 1) * block)):
+            y = y + dot(g_ref[:high, rim], ext_v[rim, :])
+        return y
+
+    def depart(ex, double, alpha, beta, y):
         now = y[: 2 * ghost, :width] + y[: 2 * ghost, width:]
         for way in range(2):
             send[ex, way, :ghost] = now[way * ghost : (way + 1) * ghost]
@@ -382,7 +442,8 @@
     def pair(ex, te):
         alpha, beta = (1.0 - OMEGA, OMEGA) if te else (C1, C2)
         gamma = OMEGA if te else C2 - 1.0
-        depart(ex, True, alpha, beta)
+        if not te:
+            depart(ex, True, alpha, beta, all_sent(True))
 
         def first(b, sl, off):
             v = xs[sl, :]
@@ -397,6 +458,10 @@
                 sol_ref[sl, :] += v + w
 
         local_apply(ext_v, first)
+        if not te:
+            @pl.when(ex == 0)
+            def _():
+                slab_passes(ends[1], ends[2])
 
         def second(b, sl, off):
             r = res_ref[sl, :] - off
@@ -407,6 +472,12 @@
 
         local_apply(ext_w, second)
         mid_product(True)
+        if not te:
+            @pl.when(ex == 0)
+            def _():
+                slab_passes(ends[2], ends[3])
+                take_slabs(0, min(2, ends[3] // CHUNKS + 1))
+
         arrive(ex, True)
         off_below, off_above = ghost_terms(ex)
         dw_below = -beta * (dinv_ref[below_rows, :] * off_below)
@@ -433,13 +504,20 @@
             ext_v[ghost + b * block : ghost + (b + 1) * block, :] = split_lanes(v)
 
     def restricted(ex):
-        depart(ex, False, 0.0, 0.0)
+        depart(ex, False, 0.0, 0.0, all_sent(False))
 
         def restrict(b, sl, off):
             s2[sl, :] = split_lanes((1.0 - OMEGA) * res_ref[sl, :] - OMEGA * off)
 
         local_apply(ext_v, restrict)
         both = dot(oht_ref[...], s2[...])
+
+        @pl.when(ex == 1)
+        def _():
+            slab_passes(ends[3], ends[4])
+            taken = min(2, ends[3] // CHUNKS + 1)
+            take_slabs(taken, max(taken, min(3, ends[4] // CHUNKS + 1)))
+
         arrive(ex, False)
         off_below, off_above = ghost_terms(ex)
         nothing = jnp.zeros((ghost, 2 * width), bf16)
@@ -449,27 +527,20 @@
         return both[:, :width] + both[:, width:]
 
     def polynomial():
-        half = parts // 2
-        eye = iota((agg, agg), 0) == iota((agg, agg), 1)
-        cinv = []
+        cinv = [cinv_ref[:, j * agg : (j + 1) * agg] for j in range(parts)]
+        first_rho = 1.0 / (2.0 * THETA / DELTA - RHO0)
+        mine_diag = own_ref[:, mine]
+        mine_inv = 1.0 / jnp.sum(jnp.where(eye, mine_diag, 0.0), axis=1, keepdims=True)
         for j in range(parts):
             sl = slice(j * agg, (j + 1) * agg)
-            cinv.append(1.0 / jnp.sum(jnp.where(eye, slabs[sl, :agg], 0.0), axis=0, keepdims=True))
-            for k in range(half + 1):
-                other = (j + k) % parts
-                so = slice(other * agg, (other + 1) * agg)
-                tile = slabs[sl, k * agg : (k + 1) * agg]
-                m_hi[sl, so], m_lo[sl, so] = split(tile)
-                if 0 < k and 2 * k < parts:
-                    m_hi[so, sl], m_lo[so, sl] = split(tile.T)
-        for j in range(parts):
-            sl = slice(j * agg, (j + 1) * agg)
-            start = jnp.where(jnp.logical_and(eye, me == j), cinv[j], 0.0)
-            pd[:, sl] = start
-            pz[:, sl] = start
-            px[:, sl] = start
-        rho_old = RHO0
-        for turn in range(1, CHEB_COARSE):
+            begin = jnp.where(jnp.logical_and(eye, me == j), cinv[j], 0.0)
+            z = begin - (mine_inv * own_ref[:, sl]) * cinv[j]
+            d = first_rho * RHO0 * begin + (2.0 * first_rho / DELTA) * z
+            pz[:, sl] = z
+            pd[:, sl] = d
+            px[:, sl] = begin + d
+        rho_old = first_rho
+        for turn in range(2, CHEB_COARSE):
             rho_new = 1.0 / (2.0 * THETA / DELTA - rho_old)
             hi, lo = split(pd[...])
             pair2[:agg, :] = hi
@@ -489,34 +560,56 @@
         m2[:agg, :] = hi
         m2[agg:, :] = lo
 
-    def gather(step):
-        half = n_sub // 2
-
-        def block_copy(source, origin, slot, peer):
-            return pltpu.make_async_remote_copy(
-                src_ref=source, dst_ref=whole.at[step, aligned(origin * agg, agg)],
-                send_sem=csend_sem.at[step, slot], recv_sem=crecv_sem.at[step, slot],
-                device_id=(grp, peer), device_id_type=MESH,
-            )
-
-        copies = [block_copy(csend.at[step], me, 0, partner)]
-        for j in range(1, half):
-            copies.append(block_copy(csend.at[step], me, j, lax.rem(me + 2 * j, n_sub)))
-        for copy in copies:
-            copy.start()
-        whole[step, mine, :] = csend[step]
-        passed = []
-        for j in range(1, half):
-            copies[j].wait_recv()
-            origin = lax.rem(me + n_sub - 2 * j, n_sub)
-            copy = block_copy(whole.at[step, aligned(origin * agg, agg)], origin, half + j, partner)
-            copy.start()
-            passed.append(copy)
-        copies[0].wait_recv()
-        for copy in passed:
-            copy.wait_recv()
-        for copy in copies + passed:
-            copy.wait_send()
+    pos = lax.div(me, 2)
+    part_rows = agg // PIECES
+
+    def coarse_copy(step, origin, c, peer, sends, recvs):
+        at = pl.ds(pl.multiple_of(origin * agg + c * part_rows, part_rows), part_rows)
+        return pltpu.make_async_remote_copy(
+            src_ref=whole.at[step, at], dst_ref=whole.at[step, at], send_sem=sends, recv_sem=recvs,
+            device_id=(grp, peer), device_id_type=MESH,
+        )
+
+    def along(step, far_by, way, c, origin):
+        peer = me + 2 * far_by if way == UP else me - 2 * far_by
+        return coarse_copy(step, origin, c, peer, line_send.at[step, way, far_by - 1, c], line_recv.at[step, way, far_by - 1, c])
+
+    def over(step, c, origin):
+        q = lax.div(origin, 2)
+        return coarse_copy(step, origin, c, partner, over_send.at[step, q, c], over_recv.at[step, q, c])
+
+    def reaches(far_by, way):
+        return pos + far_by < line if way == UP else pos - far_by >= 0
+
+    def gather_open(step):
+        for c in range(PIECES):
+            over(step, c, me).start()
+            for far_by in reversed(range(1, line)):
+                for way in (UP, DOWN):
+                    @pl.when(reaches(far_by, way))
+                    def _():
+                        along(step, far_by, way, c, me).start()
+
+    def gather_pass(step):
+        for far_by in range(1, line):
+            for c in range(PIECES):
+                for way in (UP, DOWN):
+                    @pl.when(reaches(far_by, 1 - way))
+                    def _():
+                        origin = me - 2 * far_by if way == UP else me + 2 * far_by
+                        along(step, far_by, way, c, origin).wait_recv()
+                        over(step, c, origin).start()
+
+    def gather_close(step):
+        for c in range(PIECES):
+            for q in range(line):
+                over(step, c, 2 * q + 1 - odd).wait_recv()
+                over(step, c, 2 * q + odd).wait_send()
+            for far_by in range(1, line):
+                for way in (UP, DOWN):
+                    @pl.when(reaches(far_by, way))
+                    def _():
+                        along(step, far_by, way, c, me).wait_send()
 
     for way, d in ((0, 1), (1, -1)):
         @pl.when(has[d])
@@ -543,36 +636,58 @@
                 r2[way, ghost:] = lo
 
         pair(ex, False)
-        csend[cycle] = restricted(ex + 1)
+        whole[cycle, mine, :] = restricted(ex + 1)
+        gather_open(cycle)
 
         @pl.when(cycle == 0)
         def _():
-            def rest(event, c):
-                slab_pass(event)
-                return c
-
-            lax.fori_loop(in_setup, events, rest, 0)
+            slab_passes(ends[4], events)
+
+        gather_pass(cycle)
+
+        @pl.when(cycle == 0)
+        def _():
             slab_close()
+            take_slabs(max(min(2, ends[3] // CHUNKS + 1), min(3, ends[4] // CHUNKS + 1)), line + 1)
             polynomial()
 
-        gather(cycle)
+        gather_close(cycle)
         corr = split_lanes(quads(dot(m2[...], split_lanes(whole[cycle])), agg, width))
+        depart(ex + 2, True, 1.0 - OMEGA, OMEGA, dot(go_ref[...], corr))
 
         def spread(b, c):
             sl = aligned(b * block, block)
-            both = dot(oh_ref[sl, :], corr)
+            both = dot(oh_ref[pl.ds(pl.multiple_of(ghost + b * block, ghost), block), :], corr)
             t = both[:, :width] + both[:, width:]
             xs[sl, :] = t
             store_ext(ext_v, b, t)
             return c
 
         lax.fori_loop(0, blocks, spread, 0, unroll=4)
-        mid_product(True)
         pair(ex + 2, True)
         pair(ex + 3, False)
         return carry
 
     lax.fori_loop(0, CYCLES, cycle_body, 0)
+
+
+def store_kernel(a_ref, b_ref, c_ref, d_ref, sem):
+    copies = [pltpu.make_async_copy(a_ref, c_ref, sem.at[0]), pltpu.make_async_copy(b_ref, d_ref, sem.at[1])]
+    for copy in copies:
+        copy.start()
+    for copy in copies:
+        copy.wait()
+
+
+def store(sol, res):
+    return pl.pallas_call(
+        store_kernel,
+        in_specs=[pl.BlockSpec(memory_space=pltpu.VMEM)] * 2,
+        out_specs=[pl.BlockSpec(memory_space=pltpu.HBM)] * 2,
+        out_shape=[jax.ShapeDtypeStruct(sol.shape, f32)] * 2,
+        scratch_shapes=[pltpu.SemaphoreType.DMA((2,))],
+        name="store",
+    )(sol, res)
 
 
 def body(n_grp, n_sub, right_side, fine_values, columns, agg_map, send_lo, send_hi, coarse_matrix):
@@ -587,16 +702,24 @@
     vmem = pl.BlockSpec(memory_space=pltpu.VMEM)
     field = jax.ShapeDtypeStruct((rows, width), f32)
     dma = pltpu.SemaphoreType.DMA
-    return pl.pallas_call(
+    sol, res = pl.pallas_call(
         functools.partial(kernel, n_grp, n_sub),
-        in_specs=[vmem] * 7,
+        in_specs=[pl.BlockSpec(memory_space=pltpu.HBM)] * 7,
         out_specs=[vmem] * 2,
         out_shape=[field] * 2,
         scratch_shapes=[
+            pltpu.VMEM((rows, width), f32),
+            pltpu.VMEM(fine_values.shape, f32),
+            pltpu.VMEM(columns.shape, jnp.int32),
+            pltpu.VMEM((1, rows), jnp.int32),
+            pltpu.VMEM((1, ghost), jnp.int32),
+            pltpu.VMEM((1, ghost), jnp.int32),
+            pltpu.VMEM((agg, coarse), f32),
+            dma((7,)),
             pltpu.VMEM((2 * rows, 2 * block), bf16),
             pltpu.VMEM((rows, block), f32),
             pltpu.VMEM((rows, block), f32),
-            pltpu.VMEM((rows, agg), bf16),
+            pltpu.VMEM((ext_rows, agg), bf16),
             pltpu.VMEM((agg, rows), bf16),
             pltpu.VMEM((6 * ghost, ext_rows), bf16),
             pltpu.VMEM((2 * ghost, ext_rows), f32),
@@ -619,8 +742,9 @@
             dma((2,)),
             dma((2,)),
             pltpu.VMEM((coarse, kept), f32),
-            dma((3, n_sub // 2, CHUNKS)),
-            dma((3, n_sub // 2, CHUNKS)),
+            dma((2, n_sub // 2, CHUNKS)),
+            dma((2, n_sub // 2, CHUNKS)),
+            pltpu.VMEM((1, coarse), f32),
             pltpu.VMEM((coarse, coarse), bf16),
             pltpu.VMEM((coarse, coarse), bf16),
             pltpu.VMEM((agg, coarse), f32),
@@ -628,10 +752,12 @@
             pltpu.VMEM((agg, coarse), f32),
             pltpu.VMEM((2 * agg, coarse), bf16),
             pltpu.VMEM((2 * agg, coarse), bf16),
-            pltpu.VMEM((CYCLES, agg, width), f32),
             pltpu.VMEM((CYCLES, coarse, width), f32),
-            dma((CYCLES, n_sub)),
-            dma((CYCLES, n_sub)),
+            dma((CYCLES, 2, n_sub // 2 - 1, PIECES)),
+            dma((CYCLES, 2, n_sub // 2 - 1, PIECES)),
+            dma((CYCLES, n_sub // 2, PIECES)),
+            dma((CYCLES, n_sub // 2, PIECES)),
+            pltpu.VMEM((6 * ghost, agg), bf16),
         ],
         compiler_params=pltpu.CompilerParams(
             collective_id=0, has_side_effects=True, vmem_limit_bytes=60 * 1024 * 1024
@@ -641,6 +767,7 @@
         right_side, fine_values, columns, agg_map.reshape(1, rows),
         send_lo.reshape(1, ghost), send_hi.reshape(1, ghost), own,
     )
+    return sol, res
 
 
 def solution(mesh):

time: 116 us -> 103 us (0.89)
  Pallas kernels: 112 us -> 99.2 us
    pallas_call x1, Pallas kernels: 112 us -> 99.2 us  [body(): pl.pallas_call(functools.partial(kernel, n_grp, n_sub), in_specs=[pl.Bloc...]
where the time goes in v2:
time: 103 us
  Pallas kernels  99.2 us (96%)
  local copies, waits for them, and re-layouts  3.32 us (3%)
    pallas_call x1, Pallas kernels, body(): pl.pallas_call(functools.partial(kernel, n_grp, n_sub), in_specs=[pl.Bloc...  99.2 us
    unnamed x4, local copies, waits for them, and re-layouts  3.32 us

profile of v2, /device:TPU:1, one launch (start us, length us, event | category | flops | bytes accessed | tf_op | source)
XLA Modules:
  0.0 103.2 jit_solution(4624696527333896591)
XLA Ops:
  0.6 99.2 %cycles.1 = (f32[2048,128]{1,0:T(8,128)}, f32[2048,128]{1,0:T(8,128)}) custom-call(f32[2048,128]{1,0:T(8,128)} %refs_0_.1, f32[81,2048]{1,0:T(8,128)} %refs_1_.1, s32[81,2048]{1,0:T(8,128)} %refs_2_.1, s32[1,2048]{1,0:T(1,128)} %bitcast.5, s32[1,64]{1,0:T(1,128)} %bitcast.6, s32[1,64]{1,0:T(1,128)} %bitcast.7, f32[128,1024]{1,0:T(8,128)} %bitcast.4), custom_call_target="tpu_custom_call" | custom-call | tf_op jit(solution)/shard_map/cycles/pallas_call | solution.py:705
  99.9 0.0 copy-start
  99.9 2.4 %copy.11 = f32[2048,128]{1,0:T(8,128)} copy(f32[2048,128]{1,0:T(8,128)} %get-tuple-element.4) | data formatting | bytes 2097152
  102.2 0.0 copy-done
  102.2 1.0 copy.12
Async XLA Ops:
  99.9 2.4 %copy-start = (f32[2048,128]{1,0:T(8,128)S(1)}, f32[2048,128]{1,0:T(8,128)}, u32[]{:S(2)}) copy-start(f32[2048,128]{1,0:T(8,128)} %get-tuple-element.5) | copy-start | bytes 3145732

commit v3 on v2

--- a/solution.py
+++ b/solution.py
@@ -10,7 +10,7 @@
 CHEB_COARSE = 6
 CYCLES = 2
 ROUNDS = 4
-FIRST = 1
+FIRST = 3
 CHUNKS = 4
 PIECES = 2
 
@@ -308,7 +308,7 @@
 
     lax.fori_loop(0, blocks // 2, setup, 0)
     done = min(blocks // 2 - FIRST, events)
-    ends = [done] + [min(done + n, events) for n in (2, 3, 4, 5)]
+    ends = [done] + [min(done + n, events) for n in (0, 2, 3, 5)]
 
     def sent_rows(b, carry):
         sl = aligned(b * block, block)
@@ -639,14 +639,11 @@
         whole[cycle, mine, :] = restricted(ex + 1)
         gather_open(cycle)
 
+        gather_pass(cycle)
+
         @pl.when(cycle == 0)
         def _():
             slab_passes(ends[4], events)
-
-        gather_pass(cycle)
-
-        @pl.when(cycle == 0)
-        def _():
             slab_close()
             take_slabs(max(min(2, ends[3] // CHUNKS + 1), min(3, ends[4] // CHUNKS + 1)), line + 1)
             polynomial()
@@ -687,7 +684,7 @@
         out_shape=[jax.ShapeDtypeStruct(sol.shape, f32)] * 2,
         scratch_shapes=[pltpu.SemaphoreType.DMA((2,))],
         name="store",
-    )(sol, res)
+    )(*[pltpu.with_memory_space_constraint(x, pltpu.VMEM) for x in (sol, res)])
 
 
 def body(n_grp, n_sub, right_side, fine_values, columns, agg_map, send_lo, send_hi, coarse_matrix):
@@ -760,14 +757,14 @@
             pltpu.VMEM((6 * ghost, agg), bf16),
         ],
         compiler_params=pltpu.CompilerParams(
-            collective_id=0, has_side_effects=True, vmem_limit_bytes=60 * 1024 * 1024
+            collective_id=0, has_side_effects=True, vmem_limit_bytes=min(60 * 1024 * 1024, 27 * 1024 * 1024 + 9 * coarse * coarse)
         ),
         name="cycles",
-    )(
-        right_side, fine_values, columns, agg_map.reshape(1, rows),
-        send_lo.reshape(1, ghost), send_hi.reshape(1, ghost), own,
-    )
-    return sol, res
+    )(*[
+        pltpu.with_memory_space_constraint(x, pltpu.HBM)
+        for x in (right_side, fine_values, columns, agg_map.reshape(1, rows), send_lo.reshape(1, ghost), send_hi.reshape(1, ghost), own)
+    ])
+    return store(sol, res)
 
 
 def solution(mesh):

time: 103 us -> 97.2 us (0.944); the launches traced: 103 us -> 95.9 us
  Pallas kernels: 99.2 us -> 95.1 us
  local copies, waits for them, and re-layouts: 3.32 us -> 0 us
    pallas_call x1, Pallas kernels: 99.2 us -> 93.7 us  [body(): pl.pallas_call(functools.partial(kernel, n_grp, n_sub), in_specs=[pl.Bloc...]
    unnamed x4 -> x0, local copies, waits for them, and re-layouts: 3.32 us -> none
    pallas_call x0 -> x1, Pallas kernels: none -> 1.33 us  [store(): pl.pallas_call(store_kernel, in_specs=[pl.BlockSpec(memory_space=pltpu.VM...]
where the time goes in v3:
time: 97.2 us; the launch traced here: 95.9 us
  Pallas kernels  95.1 us (98%)
    pallas_call x1, Pallas kernels, body(): pl.pallas_call(functools.partial(kernel, n_grp, n_sub), in_specs=[pl.Bloc...  93.7 us

profile of v3, /device:TPU:1, one launch (start us, length us, event | category | flops | bytes accessed | tf_op | source)
XLA Modules:
  0.0 95.9 jit_solution(16551450352991074806)
XLA Ops:
  0.6 93.7 %cycles.1 = (f32[2048,128]{1,0:T(8,128)S(1)}, f32[2048,128]{1,0:T(8,128)S(1)}) custom-call(f32[2048,128]{1,0:T(8,128)} %refs_0_.1, f32[81,2048]{1,0:T(8,128)} %refs_1_.1, s32[81,2048]{1,0:T(8,128)} %refs_2_.1, s32[1,2048]{1,0:T(1,128)} %bitcast.5, s32[1,64]{1,0:T(1,128)} %bitcast.6, s32[1,64]{1,0:T(1,128)} %bitcast.7, f32[128,1024]{1,0:T(8,128)} %bitcast.4), custom_call_target="tpu_custom_call" | custom-call | tf_op jit(solution)/shard_map/cycles/pallas_call | solution.py:702
  94.4 1.3 %store.1 = (f32[2048,128]{1,0:T(8,128)}, f32[2048,128]{1,0:T(8,128)}) custom-call(f32[2048,128]{1,0:T(8,128)S(1)} %get-tuple-element.4.a_ref, f32[2048,128]{1,0:T(8,128)S(1)} %get-tuple-element.5.b_ref), custom_call_target="tpu_custom_call" | custom-call | tf_op jit(solution)/shard_map/store/pallas_call | solution.py:680

commit v4 on v3

--- a/solution.py
+++ b/solution.py
@@ -419,7 +419,7 @@
             fn(b, aligned(b * block, block), quads(dot(a, x), block, width))
             return carry
 
-        lax.fori_loop(0, blocks, go, 0, unroll=4)
+        lax.fori_loop(0, blocks, go, 0, unroll=8)
 
     def store_ext(ext, b, x):
         ext[pl.ds(pl.multiple_of(ghost + b * block, ghost), block), :] = split_lanes(x)

time: 97.2 us -> 95.6 us (0.984); the launches traced: 95.9 us -> 95.5 us
  no operation moved by 1% of the time
where the time goes in v4:
time: 95.6 us; the launch traced here: 95.5 us
  Pallas kernels  94.7 us (99%)
    pallas_call x1, Pallas kernels, body(): pl.pallas_call(functools.partial(kernel, n_grp, n_sub), in_specs=[pl.Bloc...  93.3 us

profile of v4, /device:TPU:1, one launch (start us, length us, event | category | flops | bytes accessed | tf_op | source)
XLA Modules:
  0.0 95.5 jit_solution(8857866472962812348)
XLA Ops:
  0.6 93.3 %cycles.1 = (f32[2048,128]{1,0:T(8,128)S(1)}, f32[2048,128]{1,0:T(8,128)S(1)}) custom-call(f32[2048,128]{1,0:T(8,128)} %refs_0_.1, f32[81,2048]{1,0:T(8,128)} %refs_1_.1, s32[81,2048]{1,0:T(8,128)} %refs_2_.1, s32[1,2048]{1,0:T(1,128)} %bitcast.5, s32[1,64]{1,0:T(1,128)} %bitcast.6, s32[1,64]{1,0:T(1,128)} %bitcast.7, f32[128,1024]{1,0:T(8,128)} %bitcast.4), custom_call_target="tpu_custom_call" | custom-call | tf_op jit(solution)/shard_map/cycles/pallas_call | solution.py:702
  94.0 1.3 %store.1 = (f32[2048,128]{1,0:T(8,128)}, f32[2048,128]{1,0:T(8,128)}) custom-call(f32[2048,128]{1,0:T(8,128)S(1)} %get-tuple-element.4.a_ref, f32[2048,128]{1,0:T(8,128)S(1)} %get-tuple-element.5.b_ref), custom_call_target="tpu_custom_call" | custom-call | tf_op jit(solution)/shard_map/store/pallas_call | solution.py:680

commit v5 on v4

--- a/solution.py
+++ b/solution.py
@@ -394,23 +394,18 @@
 
     def arrive(ex, double):
         count = 2 * ghost if double else ghost
-        for way, d in ((0, 1), (1, -1)):
-            @pl.when(has[-d])
+        for way, d in ((0, -1), (1, 1)):
+            @pl.when(has[d])
             def _():
                 near_copy(ex, way, count).wait_recv()
-
-            @pl.when(has[d])
-            def _():
-                near_copy(ex, way, count).wait_send()
+                near_copy(ex, 1 - way, count).wait_send()
+
         if double:
-            for way, d in ((0, 2), (1, -2)):
-                @pl.when(has[-d])
+            for way, d in ((0, -2), (1, 2)):
+                @pl.when(has[d])
                 def _():
                     far_copy(ex, way).wait_recv()
-
-                @pl.when(has[d])
-                def _():
-                    far_copy(ex, way).wait_send()
+                    far_copy(ex, 1 - way).wait_send()
 
     def local_apply(ext, fn):
         def go(b, carry):

time: 95.6 us -> 95.6 us (level)
  no operation moved by 1% of the time
where the time goes in v5:
time: 95.6 us; the launch traced here: 95.5 us
  Pallas kernels  94.7 us (99%)
    pallas_call x1, Pallas kernels, body(): pl.pallas_call(functools.partial(kernel, n_grp, n_sub), in_specs=[pl.Bloc...  93.3 us

profile of v5, /device:TPU:1, one launch (start us, length us, event | category | flops | bytes accessed | tf_op | source)
XLA Modules:
  0.0 95.5 jit_solution(12014890914386051376)
XLA Ops:
  0.6 93.3 %cycles.1 = (f32[2048,128]{1,0:T(8,128)S(1)}, f32[2048,128]{1,0:T(8,128)S(1)}) custom-call(f32[2048,128]{1,0:T(8,128)} %refs_0_.1, f32[81,2048]{1,0:T(8,128)} %refs_1_.1, s32[81,2048]{1,0:T(8,128)} %refs_2_.1, s32[1,2048]{1,0:T(1,128)} %bitcast.5, s32[1,64]{1,0:T(1,128)} %bitcast.6, s32[1,64]{1,0:T(1,128)} %bitcast.7, f32[128,1024]{1,0:T(8,128)} %bitcast.4), custom_call_target="tpu_custom_call" | custom-call | tf_op jit(solution)/shard_map/cycles/pallas_call | solution.py:697
  94.0 1.3 %store.1 = (f32[2048,128]{1,0:T(8,128)}, f32[2048,128]{1,0:T(8,128)}) custom-call(f32[2048,128]{1,0:T(8,128)S(1)} %get-tuple-element.4.a_ref, f32[2048,128]{1,0:T(8,128)S(1)} %get-tuple-element.5.b_ref), custom_call_target="tpu_custom_call" | custom-call | tf_op jit(solution)/shard_map/store/pallas_call | solution.py:675
